TPU v7x, 32 devices: a whole 2x2x4 slice. The times are simulated.
32 devices in a mesh: ctx: 8 (over z, y), head: 4 (over x, core).
Axes of the slice: x: 2, y: 2, z: 4, core: 2. Of those that a mesh axis runs over, the one named last changes fastest.
Arguments:
- queries: bfloat16 [4096, 5120], P('ctx', 'head'), may hold values from -34 to 34
- key_rows: bfloat16 [4096, 5120], P('ctx', 'head'), may hold values from -8 to 8
- value_rows: bfloat16 [4096, 5120], P('ctx', 'head'), may hold values from -23 to 23
- learning_rates: float32 [8, 4096], P('head', 'ctx'), may hold values from 0.02 to 1
- fast_gate: bfloat16 [8, 640, 640], P('head'), may hold values from -0.25 to 0.25
- fast_lift: bfloat16 [8, 640, 640], P('head'), may hold values from -0.25 to 0.25
- fast_down: bfloat16 [8, 640, 640], P('head'), may hold values from -0.25 to 0.25
- output_gain: float32 [5120], P('head'), may hold values from 0.25 to 1.75
- output_weight: bfloat16 [5120, 5120], P(None, 'head'), may hold values from -0.078125 to 0.078125
Outputs:
- layer_output: bfloat16 [4096, 5120], P('ctx', 'head')
All inputs are finite; a program needn't handle non-finite values.
Results may differ from a plain program's by a relative error of at most 0.025.
Values may be sent and summed in bfloat16 or wider, within the bound.
No kernel may reach another device: no remote copies, remote signals or barrier semaphores. Data moves between devices by JAX's collectives and lax.ppermute only.
A program may use at most 128 MiB of HBM per device.

v0:
```python
import jax
import jax.numpy as jnp
from jax import lax
from jax.sharding import PartitionSpec as P

HD = 640
ATT_HD = 128
WINDOW = 512
NS_ITERS = 3


quintic_first = 3.4445
quintic_second = -4.775
quintic_third = 2.0315


def shifted(array, axis, by):
    size = lax.axis_size(axis)
    pairs = [(i, i + by) for i in range(size) if 0 <= i + by < size]
    return lax.ppermute(array, axis, pairs)


def settle(values):
    return lax.optimization_barrier(values.astype(jnp.bfloat16))


def silu_slope(inputs):
    logistic = jax.nn.sigmoid(inputs)
    return logistic * (1.0 + inputs * (1.0 - logistic))


def local_attention(queries, key_rows, value_rows, earlier_keys, earlier_values, device_row):
    tokens = queries.shape[0]
    heads_here = queries.shape[1] // ATT_HD
    stride = min(512, tokens)
    keys_joined = jnp.concatenate([earlier_keys, key_rows], axis=0)
    values_joined = jnp.concatenate([earlier_values, value_rows], axis=0)
    query_block = queries.reshape(stride, heads_here, ATT_HD)
    key_block = keys_joined.reshape(stride + WINDOW, heads_here, ATT_HD)
    value_block = values_joined.reshape(stride + WINDOW, heads_here, ATT_HD)
    scores = jnp.einsum(
        "qhd,khd->hqk", query_block, key_block, preferred_element_type=jnp.float32
    ) * ATT_HD ** (-0.5)
    query_place = device_row + 0 + jnp.arange(stride, dtype=jnp.int32)[:, None]
    key_place = device_row + 0 - WINDOW + jnp.arange(stride + WINDOW, dtype=jnp.int32)[None, :]
    allowed = (key_place > query_place - WINDOW) & (key_place <= query_place) & (key_place >= 0)
    scores = jnp.where(allowed[None], scores, -1e30)
    row_peak = jnp.max(scores, axis=2, keepdims=True)
    weights = jnp.exp(scores - row_peak)
    row_total = jnp.sum(weights, axis=2, keepdims=True)
    probabilities = (weights / row_total).astype(jnp.bfloat16)
    block_out = jnp.einsum(
        "hqk,khd->qhd", probabilities, value_block, preferred_element_type=jnp.float32
    )
    outputs = block_out.reshape(stride, heads_here * ATT_HD)
    return outputs


def on_device(
    queries,
    key_rows,
    value_rows,
    learning_rates,
    fast_gate,
    fast_lift,
    fast_down,
    output_gain,
    output_weight,
):
    tokens = queries.shape[0]
    heads_here = queries.shape[1] // HD
    device_row = lax.axis_index("ctx") * tokens
    earlier_keys, earlier_values = shifted((key_rows, value_rows), "ctx", 1)
    attended = local_attention(
        queries, key_rows, value_rows, earlier_keys, earlier_values, device_row
    )
    attended = attended.reshape(tokens, heads_here, HD)
    key_heads = key_rows.reshape(tokens, heads_here, HD)
    gate_pre = jnp.einsum("thd,hde->the", key_heads, fast_gate, preferred_element_type=jnp.float32)
    lift_pre = jnp.einsum("thd,hde->the", key_heads, fast_lift, preferred_element_type=jnp.float32)
    hidden = (jax.nn.silu(gate_pre) * lift_pre).astype(jnp.bfloat16)
    token_rates = jnp.transpose(learning_rates)
    scaled = (
        token_rates[:, :, None] * value_rows.reshape(tokens, heads_here, HD).astype(jnp.float32)
    ).astype(jnp.bfloat16)
    backward = jnp.einsum("thd,hed->the", scaled, fast_down, preferred_element_type=jnp.float32)
    grad_gate = (backward * lift_pre * silu_slope(gate_pre)).astype(jnp.bfloat16)
    grad_lift = (backward * jax.nn.silu(gate_pre)).astype(jnp.bfloat16)
    partial_gate = jnp.einsum(
        "thd,the->hde", key_heads, grad_gate, preferred_element_type=jnp.float32
    )
    partial_lift = jnp.einsum(
        "thd,the->hde", key_heads, grad_lift, preferred_element_type=jnp.float32
    )
    partial_down = jnp.einsum("the,thd->hed", hidden, scaled, preferred_element_type=jnp.float32)
    partials = jnp.stack([partial_gate, partial_lift, partial_down], axis=1).reshape(
        3 * heads_here, HD, HD
    )
    summed = lax.psum(partials.astype(jnp.bfloat16), "ctx").astype(jnp.float32)
    squares = jnp.sum(summed * summed, axis=(1, 2))
    iterate_full = settle(summed / (jnp.sqrt(squares)[:, None, None] + 1e-06))
    for iteration in range(NS_ITERS):
        gram_full = settle(
            jnp.einsum(
                "mrd,med->mre", iterate_full, iterate_full, preferred_element_type=jnp.float32
            )
        )
        product_full = settle(
            jnp.einsum("mre,med->mrd", gram_full, iterate_full, preferred_element_type=jnp.float32)
        )
        second_full = jnp.einsum(
            "mre,med->mrd", gram_full, product_full, preferred_element_type=jnp.float32
        )
        iterate_full = settle(
            quintic_first * iterate_full.astype(jnp.float32)
            + quintic_second * product_full.astype(jnp.float32)
            + quintic_third * second_full
        )
    initial = (
        jnp.stack([fast_gate, fast_lift, fast_down], axis=1)
        .reshape(3 * heads_here, HD, HD)
        .astype(jnp.float32)
    )
    updated = initial + iterate_full.astype(jnp.float32)
    target = jnp.sqrt(jnp.sum(initial * initial, axis=1, keepdims=True))
    current = jnp.sqrt(jnp.sum(updated * updated, axis=1, keepdims=True) + 1e-06)
    renewed = (updated * (target / current)).astype(jnp.bfloat16).reshape(heads_here, 3, HD, HD)
    query_heads = queries.reshape(tokens, heads_here, HD)
    applied_gate = jnp.einsum(
        "thd,hde->the", query_heads, renewed[:, 0], preferred_element_type=jnp.float32
    )
    applied_lift = jnp.einsum(
        "thd,hde->the", query_heads, renewed[:, 1], preferred_element_type=jnp.float32
    )
    applied_hidden = (jax.nn.silu(applied_gate) * applied_lift).astype(jnp.bfloat16)
    fast_result = jnp.einsum(
        "the,hed->thd", applied_hidden, renewed[:, 2], preferred_element_type=jnp.float32
    )
    scale_back = lax.rsqrt(jnp.mean(fast_result * fast_result, axis=2, keepdims=True) + 1e-06)
    normed = fast_result * scale_back * output_gain.reshape(heads_here, HD)[None]
    combined = (attended + normed).astype(jnp.bfloat16).reshape(tokens, heads_here * HD)
    projected = jnp.dot(
        lax.all_gather(combined, "head", axis=1, tiled=True),
        output_weight,
        preferred_element_type=jnp.float32,
    )
    return projected.astype(jnp.bfloat16)


def solution(mesh):
    return jax.shard_map(
        on_device,
        mesh=mesh,
        in_specs=(
            P("ctx", "head"),
            P("ctx", "head"),
            P("ctx", "head"),
            P("head", "ctx"),
            P("head", None, None),
            P("head", None, None),
            P("head", None, None),
            P("head"),
            P(None, "head"),
        ),
        out_specs=P("ctx", "head"),
        check_vma=False,
    )
```

profile of v0, /device:TPU:0, one launch (start us, length us, event | category | flops | bytes accessed | tf_op | source)
XLA Modules:
  0.0 407.2 jit_solution(16960712276331299279)
XLA Ops:
  6.5 6.1 %collective-permute-start = (bf16[512,1280]{1,0:T(8,128)(2,1)}, bf16[512,1280]{1,0:T(8,128)(2,1)}, u32[]{:S(2)}, u32[]{:S(2)}) collective-permute-start(bf16[512,1280]{1,0:T(8,128)(2,1)} %param.11), channel_id=1, source_target_pairs={{0,4},{4,8},{8,12},{12,16},{16,20},{20,24},{24,28},{1,5},{5,9},{9,... | collective-permute-start | bytes 3932168 | tf_op jit(solution)/shard_map/ppermute | solution.py:20
  15.0 3.7 collective-permute-start.1
  33.3 8.2 %copy.78 = bf16[2,3,640,640]{3,2,1,0:T(8,128)(2,1)} copy(bf16[2,3,640,640]{2,3,0,1:T(8,128)(2,1)} %pad_maximum_fusion) | data formatting | bytes 9830400 | tf_op jit(solution)/shard_map/stack | solution.py:96
  42.2 6.7 %maximum_convert_fusion = f32[2,3,640,640]{3,2,0,1:T(8,128)} fusion(bf16[2,1,640,640]{3,2,0,1:T(8,128)(2,1)} %bitcast.200, bf16[2,1,640,640]{3,2,0,1:T(8,128)(2,1)S(1)} %bitcast.196, bf16[2,1,640,640]{3,2,0,1:T(8,128)(2,1)S(1)} %bitcast.198), kind=kLoop, calls=%fused_computation.21 | loop fusion | flops 7372800 | bytes 14745600 | tf_op jit(solution)/shard_map/convert_element_type | solution.py:122
  52.4 8.2 %copy.64 = f32[2,3,640,640]{3,2,1,0:T(8,128)} copy(f32[2,3,640,640]{3,2,0,1:T(8,128)} %maximum_convert_fusion) | data formatting | bytes 19660800 | tf_op jit(solution)/shard_map/convert_element_type | solution.py:122
  66.2 19.3 %collective-permute-done.1 = bf16[512,1280]{0,1:T(8,128)(2,1)} collective-permute-done((bf16[512,1280]{0,1:T(8,128)(2,1)}, bf16[512,1280]{0,1:T(8,128)(2,1)}, u32[]{:S(2)}, u32[]{:S(2)}) %collective-permute-start.1) | collective-permute-done | bytes 1310752 | tf_op jit(solution)/shard_map/ppermute | solution.py:20
  89.0 13.8 %fusion.62 = (f32[10,512]{1,0:T(8,128)S(1)}, f32[10,512,1024]{1,2,0:T(8,128)}) fusion(pred[512,1024]{0,1:T(8,128)(4,1)S(1)} %and_and_fusion, bf16[1024,10,128]{0,2,1:T(8,128)(2,1)} %bitcast.213, bf16[512,10,128]{0,2,1:T(8,128)(2,1)} %bitcast.216), kind=kOutput, calls=%fused_computation.103 | convolution fusion | flops 1363149824 | bytes 25448448 | tf_op jit(solution)/shard_map/sub | solution.py:49
  102.8 10.2 %fusion.5 = f32[10,128,512]{2,1,0:T(8,128)} fusion(bf16[1024,10,128]{0,2,1:T(8,128)(2,1)S(1)} %bitcast.212, f32[10,512,1024]{1,2,0:T(8,128)} %get-tuple-element.6, f32[10,512]{1,0:T(8,128)S(1)} %get-tuple-element.5), kind=kOutput, calls=%fused_computation.10 | convolution fusion | flops 1352663040 | bytes 26234880 | tf_op jit(solution)/shard_map/hqk,khd->qhd/dot_general | solution.py:52
  113.0 124.1 %all-reduce.2.cloned.1.call-done = bf16[6,640,640]{2,1,0:T(8,128)(2,1)} async-done(((bf16[6,640,640]{2,1,0:T(8,128)(2,1)}), bf16[6,640,640]{2,1,0:T(8,128)(2,1)}) %all-reduce.2.cloned.1.call-update) | async-done | bytes 4915216 | tf_op jit(solution)/shard_map/psum | solution.py:99
  237.1 3.7 fusion.6
  242.3 4.9 %convolution_convert_fusion.6 = bf16[6,640,640]{2,1,0:T(8,128)(2,1)S(1)} fusion(bf16[6,640,640]{2,1,0:T(8,128)(2,1)S(1)} %fusion.7), kind=kOutput, calls=%fused_computation.29 | convolution fusion | flops 3148185600 | bytes 9830400 | tf_op jit(solution)/shard_map/mrd,med->mre/dot_general | solution.py:104
  249.5 6.1 %convolution_convert_fusion.5 = bf16[6,640,640]{2,1,0:T(8,128)(2,1)} fusion(bf16[6,640,640]{2,1,0:T(8,128)(2,1)S(1)} %convolution_convert_fusion.6, bf16[6,640,640]{2,1,0:T(8,128)(2,1)S(1)} %fusion.7), kind=kOutput, calls=%fused_computation.28 | convolution fusion | flops 3148185600 | bytes 14745600 | tf_op jit(solution)/shard_map/mre,med->mrd/dot_general | solution.py:109
  255.6 9.9 %add_convert_fusion.2 = bf16[6,640,640]{2,1,0:T(8,128)(2,1)S(1)} fusion(bf16[6,640,640]{2,1,0:T(8,128)(2,1)} %convolution_convert_fusion.5, bf16[6,640,640]{2,1,0:T(8,128)(2,1)S(1)} %fusion.7, bf16[6,640,640]{2,1,0:T(8,128)(2,1)} %copy-done.13), kind=kOutput, calls=%fused_computation.19 | convolution fusion | flops 3165388800 | bytes 19660800 | tf_op jit(solution)/shard_map/mre,med->mrd/dot_general | solution.py:111
  265.5 4.7 %convolution_convert_fusion.4 = bf16[6,640,640]{2,1,0:T(8,128)(2,1)S(1)} fusion(bf16[6,640,640]{2,1,0:T(8,128)(2,1)S(1)} %add_convert_fusion.2), kind=kOutput, calls=%fused_computation.27 | convolution fusion | flops 3148185600 | bytes 9830400 | tf_op jit(solution)/shard_map/mrd,med->mre/dot_general | solution.py:104
  272.5 6.4 %convolution_convert_fusion.3 = bf16[6,640,640]{2,1,0:T(8,128)(2,1)} fusion(bf16[6,640,640]{2,1,0:T(8,128)(2,1)S(1)} %convolution_convert_fusion.4, bf16[6,640,640]{2,1,0:T(8,128)(2,1)S(1)} %add_convert_fusion.2), kind=kOutput, calls=%fused_computation.26 | convolution fusion | flops 3148185600 | bytes 14745600 | tf_op jit(solution)/shard_map/mre,med->mrd/dot_general | solution.py:109
  278.9 9.9 %add_convert_fusion.1 = bf16[6,640,640]{2,1,0:T(8,128)(2,1)S(1)} fusion(bf16[6,640,640]{2,1,0:T(8,128)(2,1)} %convolution_convert_fusion.3, bf16[6,640,640]{2,1,0:T(8,128)(2,1)S(1)} %add_convert_fusion.2, bf16[6,640,640]{2,1,0:T(8,128)(2,1)} %copy-done.14), kind=kOutput, calls=%fused_computation.18 | convolution fusion | flops 3165388800 | bytes 19660800 | tf_op jit(solution)/shard_map/mre,med->mrd/dot_general | solution.py:111
  291.1 4.7 %convolution_convert_fusion.2 = bf16[6,640,640]{2,1,0:T(8,128)(2,1)S(1)} fusion(bf16[6,640,640]{2,1,0:T(8,128)(2,1)S(1)} %add_convert_fusion.1), kind=kOutput, calls=%fused_computation.25 | convolution fusion | flops 3148185600 | bytes 9830400 | tf_op jit(solution)/shard_map/mrd,med->mre/dot_general | solution.py:104
  298.0 8.9 %convolution_convert_fusion.1 = bf16[6,640,640]{2,1,0:T(8,128)(2,1)} fusion(bf16[6,640,640]{2,1,0:T(8,128)(2,1)S(1)} %convolution_convert_fusion.2, bf16[6,640,640]{2,1,0:T(8,128)(2,1)} %copy-done.12), kind=kOutput, calls=%fused_computation.24 | convolution fusion | flops 3148185600 | bytes 14745600 | tf_op jit(solution)/shard_map/mre,med->mrd/dot_general | solution.py:109
  306.9 13.6 %add_convert_fusion = bf16[6,640,640]{2,1,0:T(8,128)(2,1)} fusion(bf16[6,640,640]{2,1,0:T(8,128)(2,1)} %convolution_convert_fusion.1, bf16[6,640,640]{2,1,0:T(8,128)(2,1)} %copy-done.12, bf16[6,640,640]{2,1,0:T(8,128)(2,1)} %copy-done.15), kind=kOutput, calls=%fused_computation.17 | convolution fusion | flops 3165388800 | bytes 19660800 | tf_op jit(solution)/shard_map/mre,med->mrd/dot_general | solution.py:111
  320.6 3.7 multiply_reduce_fusion
  324.3 6.6 %multiply_convert_fusion = bf16[6,640,640]{2,1,0:T(8,128)(2,1)S(1)} fusion(bf16[6,640,640]{2,1,0:T(8,128)(2,1)} %add_convert_fusion, f32[2,3,640,640]{3,2,1,0:T(8,128)} %copy.64, f32[6,640]{1,0:T(8,128)S(1)} %rsqrt_multiply_fusion), kind=kLoop, calls=%fused_computation.14 | loop fusion | flops 9830400 | bytes 19676160 | tf_op jit(solution)/shard_map/convert_element_type | solution.py:127
  336.0 7.3 %fusion.11 = (f32[512,2]{0,1:T(2,128)S(1)}, f32[2,640,512]{2,1,0:T(8,128)}) fusion(f32[2,640,512]{1,2,0:T(8,128)} %fusion.28, bf16[2,3,640,640]{3,2,1,0:T(8,128)(2,1)} %bitcast.210, bf16[64,2,8,640]{3,2,1,0:T(8,128)(2,1)} %bitcast.214), kind=kOutput, calls=%fused_computation.36 | convolution fusion | flops 1682963456 | bytes 9834496 | tf_op jit(solution)/shard_map/the,hed->thd/dot_general | solution.py:136
  346.5 39.6 %all-gather.2.cloned.1.call-done = bf16[512,5120]{0,1:T(8,128)(2,1)} async-done(((bf16[512,1280]{0,1:T(8,128)(2,1)}), bf16[512,5120]{0,1:T(8,128)(2,1)}) %all-gather.2.cloned.1.call-update) | async-done | bytes 5242896 | tf_op jit(solution)/shard_map/all_gather | solution.py:143
  386.1 13.8 %convolution_convert_fusion = bf16[512,1280]{1,0:T(8,128)(2,1)} fusion(bf16[512,5120]{0,1:T(8,128)(2,1)} %all-gather.2.cloned.1.call-done, bf16[5120,1280]{1,0:T(8,128)(2,1)} %param.17), kind=kOutput, calls=%fused_computation.23 | convolution fusion | flops 6711541760 | bytes 19660800 | tf_op jit(solution)/shard_map/dot_general | solution.py:142
  (72 shorter events, 48.7 us)
Async XLA Ops:
  6.5 13.7 %copy-start.1 = (bf16[2,640,640]{2,1,0:T(8,128)(2,1)S(1)}, bf16[2,640,640]{2,1,0:T(8,128)(2,1)}, u32[]{:S(2)}) copy-start(bf16[2,640,640]{2,1,0:T(8,128)(2,1)} %param.14) | copy-start | bytes 4915204
  6.5 230.5 %all-reduce.2.cloned.1.call-start = ((), (), s32[]{:S(2)}) async-start(), calls=%async_computation | async-start | bytes 9830400 | tf_op jit(solution)/shard_map/psum | solution.py:99
  6.5 55.0 %collective-permute-start = (bf16[512,1280]{1,0:T(8,128)(2,1)}, bf16[512,1280]{1,0:T(8,128)(2,1)}, u32[]{:S(2)}, u32[]{:S(2)}) collective-permute-start(bf16[512,1280]{1,0:T(8,128)(2,1)} %param.11), channel_id=1, source_target_pairs={{0,4},{4,8},{8,12},{12,16},{16,20},{20,24},{24,28},{1,5},{5,9},{9,... | collective-permute-start | bytes 3932168 | tf_op jit(solution)/shard_map/ppermute | solution.py:20
  15.0 8.0 %copy-start.2 = (bf16[2,640,640]{2,1,0:T(8,128)(2,1)S(1)}, bf16[2,640,640]{2,1,0:T(8,128)(2,1)}, u32[]{:S(2)}) copy-start(bf16[2,640,640]{2,1,0:T(8,128)(2,1)} %param.13) | copy-start | bytes 4915204
  15.0 8.0 %copy-start.5 = (bf16[512,1280]{1,0:T(8,128)(2,1)S(1)}, bf16[512,1280]{1,0:T(8,128)(2,1)}, u32[]{:S(2)}) copy-start(bf16[512,1280]{1,0:T(8,128)(2,1)} %param.10) | copy-start | bytes 3932164
  15.0 70.5 %collective-permute-start.1 = (bf16[512,1280]{0,1:T(8,128)(2,1)}, bf16[512,1280]{0,1:T(8,128)(2,1)}, u32[]{:S(2)}, u32[]{:S(2)}) collective-permute-start(bf16[512,1280]{0,1:T(8,128)(2,1)} %copy.58), channel_id=1, source_target_pairs={{0,4},{4,8},{8,12},{12,16},{16,20},{20,24},{24,28},{1,5},{5,9},{9,... | collective-permute-start | bytes 3932168 | tf_op jit(solution)/shard_map/ppermute | solution.py:20
  20.2 4.1 %copy-start.3 = (bf16[2,640,640]{2,1,0:T(8,128)(2,1)S(1)}, bf16[2,640,640]{2,1,0:T(8,128)(2,1)}, u32[]{:S(2)}) copy-start(bf16[2,640,640]{2,1,0:T(8,128)(2,1)} %param.15) | copy-start | bytes 4915204
  20.2 4.1 %copy-start.11 = (f32[2,512]{1,0:T(2,128)S(1)}, f32[2,512]{1,0:T(2,128)}, u32[]{:S(2)}) copy-start(f32[2,512]{1,0:T(2,128)} %param.12) | copy-start | bytes 12292
  41.6 344.5 %all-gather.2.cloned.1.call-start = ((), (), s32[]{:S(2)}) async-start(), calls=%async_computation.1 | async-start | bytes 6553600 | tf_op jit(solution)/shard_map/all_gather | solution.py:143
  42.1 6.7 %copy-start.4 = (bf16[2,640,640]{2,1,0:T(8,128)(2,1)S(1)}, bf16[2,640,640]{2,1,0:T(8,128)(2,1)}, u32[]{:S(2)}) copy-start(bf16[2,640,640]{2,1,0:T(8,128)(2,1)} %param.15) | copy-start | bytes 4915204
  52.4 8.3 %copy-start.10 = (f32[1280]{0:T(1024)S(1)}, f32[1280]{0:T(1024)}, u32[]{:S(2)}) copy-start(f32[1280]{0:T(1024)} %param.16) | copy-start | bytes 15364
  89.0 13.8 %copy-start.8 = (bf16[1024,1280]{0,1:T(8,128)(2,1)S(1)}, bf16[1024,1280]{0,1:T(8,128)(2,1)}, u32[]{:S(2)}) copy-start(bf16[1024,1280]{0,1:T(8,128)(2,1)} %copy.57) | copy-start | bytes 7864324
  237.1 3.9 copy-start
  247.2 2.2 copy-start.13
  270.3 2.2 copy-start.14
  288.8 2.2 copy-start.12
  295.8 2.2 copy-start.15
  298.0 22.6 %slice-start = ((s8[9830400]{0:T(1024)(128)(4,1)}), s8[4194304]{0:T(1024)(128)(4,1)S(1)}, s32[]{:S(2)}) async-start(s8[9830400]{0:T(1024)(128)(4,1)} %bitcast.193), calls=%async_computation.2 | async-start | bytes 8388608
  306.9 13.7 %slice-start.1 = ((s8[9830400]{0:T(1024)(128)(4,1)}), s8[4194304]{0:T(1024)(128)(4,1)S(1)}, s32[]{:S(2)}) async-start(s8[9830400]{0:T(1024)(128)(4,1)} %bitcast.193), calls=%async_computation.3 | async-start | bytes 8388608
  306.9 13.7 %slice-start.2 = ((s8[9830400]{0:T(1024)(128)(4,1)}), s8[1441792]{0:T(1024)(128)(4,1)S(1)}, s32[]{:S(2)}) async-start(s8[9830400]{0:T(1024)(128)(4,1)} %bitcast.193), calls=%async_computation.4 | async-start | bytes 2883584
  324.3 8.8 %copy-start.9 = (bf16[512,1280]{1,0:T(8,128)(2,1)S(1)}, bf16[512,1280]{1,0:T(8,128)(2,1)}, u32[]{:S(2)}) copy-start(bf16[512,1280]{1,0:T(8,128)(2,1)} %param.9) | copy-start | bytes 3932164
  330.9 2.2 copy-start.6
  336.0 7.3 %copy-start.7 = (f32[10,128,512]{2,1,0:T(8,128)S(1)}, f32[10,128,512]{2,1,0:T(8,128)}, u32[]{:S(2)}) copy-start(f32[10,128,512]{2,1,0:T(8,128)} %fusion.5) | copy-start | bytes 7864324
Sparse Core Ops, SparseCore 0:
  41.7 195.3 all-reduce.1
  346.6 39.4 all-gather.1
where the time goes:
time: 414 us; the launch traced here: 407 us
  waiting for transfers between devices  183 us (44%)
  matrix products  127 us (31%)
  other arithmetic  36.9 us (9%)
  local copies, waits for them, and re-layouts  35.4 us (9%)
  between operations  14.3 us (3%)
  starting transfers between devices  10.3 us (2%)
    psum x1, waiting for transfers between devices, on_device(): summed = lax.psum(partials.astype(jnp.bfloat16), 'ctx').astype(jnp.float32)  124 us
    all_gather x1, waiting for transfers between devices, on_device(): lax.all_gather(combined, 'head', axis=1, tiled=True)  39.6 us
    dot_general x3, matrix products, on_device(): jnp.einsum('mre,med->mrd', gram_full, product_full, preferred_element_typ...  33.5 us
    dot_general x3, matrix products, on_device(): jnp.einsum('mre,med->mrd', gram_full, iterate_full, preferred_element_typ...  21.4 us
    ppermute x2, waiting for transfers between devices, shifted(): return lax.ppermute(array, axis, pairs)  19.3 us
    unnamed x40, local copies, waits for them, and re-layouts  16.1 us
    dot_general x3, matrix products, on_device(): jnp.einsum('mrd,med->mre', iterate_full, iterate_full, preferred_element_...  14.4 us
    dot_general x1, matrix products, on_device(): jnp.dot(lax.all_gather(combined, 'head', axis=1, tiled=True), output_weig...  13.8 us
  transfers between devices with their start and end apart: 4, of which 3 were waited for; matrix products, arithmetic and copies ran while one was open for 19% of the time, Pallas kernels for 0%

commit v1 on v0

v1 whole, which is shorter than its diff:
```python
import functools
import math

import jax
import jax.numpy as jnp
from jax import lax
from jax.experimental import pallas as pl
from jax.experimental.pallas import tpu as pltpu
from jax.sharding import PartitionSpec as P

ATT_HD = 128
WINDOW = 512
NS_ITERS = 3
PIECES = 2
VMEM_BYTES = 56 * 1024 * 1024

quintic_first = 3.4445
quintic_second = -4.775
quintic_third = 2.0315

f32 = jnp.float32
bf16 = jnp.bfloat16


def mm(a, b, dims=((1,), (0,))):
    return lax.dot_general(a, b, (dims, ((), ())), preferred_element_type=f32)


def after(value, *earlier):
    return lax.optimization_barrier((value, *earlier))[0]


def pick(blocks, which):
    out = blocks[0]
    for number in range(1, len(blocks)):
        out = jnp.where(which == number, blocks[number], out)
    return out


def tree_low(low, high):
    levels, step = [], 1
    while step < high - low:
        levels.append(
            [(i + step, i) for i in range(low, high, 2 * step) if i + step < high]
        )
        step *= 2
    return levels


def tree_high(low, high):
    return [
        [(low + high - 1 - a, low + high - 1 - b) for a, b in level]
        for level in tree_low(low, high)
    ]


def tree_mid(count):
    middle = count // 2
    left, right = tree_high(0, middle), tree_low(middle, count)
    levels = []
    for k in range(max(len(left), len(right))):
        levels.append((left[k] if k < len(left) else []) + (right[k] if k < len(right) else []))
    return levels + [[(middle - 1, middle)]]


def attention_kernel(first_ref, q_ref, kp_ref, k_ref, vp_ref, v_ref, out_ref, k_all, v_all):
    tokens = q_ref.shape[0]
    tile = ATT_HD
    span = WINDOW + tile
    k_all[:WINDOW] = kp_ref[...]
    k_all[WINDOW:] = k_ref[...]
    v_all[:WINDOW] = vp_ref[...]
    v_all[WINDOW:] = v_ref[...]
    is_first = first_ref[0] == 0
    row = lax.broadcasted_iota(jnp.int32, (tile, span), 0)
    col = lax.broadcasted_iota(jnp.int32, (tile, span), 1)
    allowed = (col > row) & (col <= row + WINDOW)
    scale = ATT_HD**-0.5 * math.log2(math.e)
    for number in range(tokens // tile):
        start = number * tile
        s = mm(q_ref[start : start + tile], k_all[start : start + span], ((1,), (1,))) * scale
        keep = allowed
        if start < WINDOW:
            keep = keep & ((col >= WINDOW - start) | jnp.logical_not(is_first))
        s = jnp.where(keep, s, -1e30)
        w = jnp.exp2(s - jnp.max(s, axis=1, keepdims=True))
        total = jnp.sum(w, axis=1, keepdims=True)
        o = mm(w.astype(bf16), v_all[start : start + span])
        out_ref[start : start + tile] = o / total


def attention(q, kp, k, vp, v, plane):
    tokens, width = q.shape
    wide = pl.BlockSpec((tokens, ATT_HD), lambda a, s: (0, a))
    before = pl.BlockSpec((WINDOW, ATT_HD), lambda a, s: (0, a))
    return pl.pallas_call(
        attention_kernel,
        out_shape=jax.ShapeDtypeStruct((tokens, width), f32),
        grid_spec=pltpu.PrefetchScalarGridSpec(
            num_scalar_prefetch=1,
            grid=(width // ATT_HD,),
            in_specs=[wide, before, wide, before, wide],
            out_specs=wide,
            scratch_shapes=[pltpu.VMEM((WINDOW + tokens, ATT_HD), bf16)] * 2,
        ),
        compiler_params=pltpu.CompilerParams(vmem_limit_bytes=VMEM_BYTES),
        cost_estimate=pl.CostEstimate(
            flops=4 * tokens * (WINDOW + ATT_HD) * width,
            bytes_accessed=12 * tokens * width,
            transcendentals=tokens * (WINDOW + ATT_HD) * (width // ATT_HD),
        ),
    )(jnp.reshape(plane, (1,)).astype(jnp.int32), q, kp, k, vp, v)


def settle_kernel(grad_ref, init_ref, out_ref, x_ref):
    g = grad_ref[...]
    square = jnp.sum(jnp.sum(g * g, axis=0, keepdims=True), axis=1, keepdims=True)
    x_ref[...] = (g / (jnp.sqrt(square) + 1e-06)).astype(bf16)

    @pl.loop(0, NS_ITERS)
    def _(_):
        x = x_ref[...]
        gram = mm(x, x, ((1,), (1,))).astype(bf16)
        product = mm(gram, x).astype(bf16)
        second = mm(gram, product)
        x_ref[...] = (
            quintic_first * x.astype(f32)
            + quintic_second * product.astype(f32)
            + quintic_third * second
        ).astype(bf16)

    initial = init_ref[...].astype(f32)
    updated = initial + x_ref[...].astype(f32)
    target = jnp.sqrt(jnp.sum(initial * initial, axis=0, keepdims=True))
    current = jnp.sqrt(jnp.sum(updated * updated, axis=0, keepdims=True) + 1e-06)
    out_ref[...] = (updated * (target / current)).astype(bf16)


def renew(gradient, initial):
    rows, columns = gradient.shape
    return pl.pallas_call(
        settle_kernel,
        out_shape=jax.ShapeDtypeStruct((rows, columns), bf16),
        scratch_shapes=[pltpu.VMEM((rows, columns), bf16)],
        compiler_params=pltpu.CompilerParams(vmem_limit_bytes=VMEM_BYTES),
        cost_estimate=pl.CostEstimate(
            flops=6 * NS_ITERS * rows * rows * columns,
            bytes_accessed=8 * rows * columns,
            transcendentals=0,
        ),
    )(gradient, initial)


def apply_kernel(which_ref, q_ref, gate_ref, lift_ref, down_ref, att_ref, gain_ref, out_ref):
    q = q_ref[...]
    gate = mm(q, gate_ref[...])
    lift = mm(q, lift_ref[...])
    hidden = (gate / (1.0 + jnp.exp(-gate)) * lift).astype(bf16)
    result = mm(hidden, down_ref[...])
    scale = lax.rsqrt(jnp.mean(result * result, axis=1, keepdims=True) + 1e-06)
    out_ref[...] = (att_ref[...] + result * scale * gain_ref[...]).astype(bf16)


def apply_fast(q, gate, lift, down, attended, gain, which):
    tokens, width = q.shape
    rows = min(256, tokens)
    blocks = tokens // rows
    whole = pl.BlockSpec((width, width), lambda i, s: (0, 0))
    return pl.pallas_call(
        apply_kernel,
        out_shape=jax.ShapeDtypeStruct((tokens, width), bf16),
        grid_spec=pltpu.PrefetchScalarGridSpec(
            num_scalar_prefetch=1,
            grid=(blocks,),
            in_specs=[
                pl.BlockSpec((rows, width), lambda i, s: (i, 0)),
                whole,
                whole,
                whole,
                pl.BlockSpec((rows, width), lambda i, s: (s[0] * blocks + i, 0)),
                pl.BlockSpec((1, width), lambda i, s: (0, 0)),
            ],
            out_specs=pl.BlockSpec((rows, width), lambda i, s: (i, 0)),
        ),
        compiler_params=pltpu.CompilerParams(vmem_limit_bytes=VMEM_BYTES),
        cost_estimate=pl.CostEstimate(
            flops=6 * tokens * width * width,
            bytes_accessed=10 * tokens * width + 6 * width * width,
            transcendentals=tokens * width,
        ),
    )(jnp.reshape(which, (1,)).astype(jnp.int32), q, gate, lift, down, attended, gain)


def project_kernel(count, has_total, is_last, *refs):
    chunk_refs = refs[1 : 1 + count]
    w_ref = refs[1 + count]
    total_ref = refs[2 + count] if has_total else None
    out_ref, sum_ref = refs[-2:]
    step = pl.program_id(0)
    for number in range(count):

        @pl.when(step == number)
        def _(number=number):
            part = mm(chunk_refs[number][...], w_ref[...])
            if number > 0:
                part += sum_ref[...]
            elif has_total:
                part += total_ref[...]
            if number == count - 1:
                out_ref[...] = part.astype(out_ref.dtype)
            else:
                sum_ref[...] = part


def project(chunks, places, weight, total, is_last):
    count = len(chunks)
    tokens, depth = chunks[0].shape
    columns = weight.shape[1]
    fixed = pl.BlockSpec((tokens, depth), lambda k, s: (0, 0))
    square = pl.BlockSpec((tokens, columns), lambda k, s: (0, 0))
    operands = list(chunks) + [weight]
    specs = [fixed] * count + [pl.BlockSpec((depth, columns), lambda k, s: (s[k], 0))]
    if total is not None:
        operands.append(total)
        specs.append(square)
    return pl.pallas_call(
        functools.partial(project_kernel, count, total is not None, is_last),
        out_shape=jax.ShapeDtypeStruct((tokens, columns), bf16 if is_last else f32),
        grid_spec=pltpu.PrefetchScalarGridSpec(
            num_scalar_prefetch=1,
            grid=(count,),
            in_specs=specs,
            out_specs=square,
            scratch_shapes=[pltpu.VMEM((tokens, columns), f32)],
        ),
        compiler_params=pltpu.CompilerParams(vmem_limit_bytes=VMEM_BYTES),
        cost_estimate=pl.CostEstimate(
            flops=2 * count * tokens * depth * columns,
            bytes_accessed=2 * count * (tokens + columns) * depth + 8 * tokens * columns,
            transcendentals=0,
        ),
    )(jnp.stack(places).astype(jnp.int32), *operands)


def token_gradients(keys, values, rates, gate, lift, down):
    gate_pre = mm(keys, gate)
    lift_pre = mm(keys, lift)
    logistic = jax.nn.sigmoid(gate_pre)
    silu = gate_pre * logistic
    hidden = (silu * lift_pre).astype(bf16)
    scaled = (rates[:, None] * values.astype(f32)).astype(bf16)
    backward = mm(scaled, down, ((1,), (1,)))
    grad_gate = (backward * lift_pre * (logistic * (1.0 + gate_pre * (1.0 - logistic)))).astype(bf16)
    grad_lift = (backward * silu).astype(bf16)
    over_tokens = ((0,), (0,))
    return (
        mm(keys, grad_gate, over_tokens),
        mm(keys, grad_lift, over_tokens),
        mm(hidden, scaled, over_tokens),
    )


def on_device(
    queries,
    key_rows,
    value_rows,
    learning_rates,
    fast_gate,
    fast_lift,
    fast_down,
    output_gain,
    output_weight,
):
    tokens = queries.shape[0]
    group, width = fast_gate.shape[0], fast_gate.shape[1]
    context = lax.axis_size("ctx")
    columns_of = lax.axis_size("head")
    planes = context // group
    place = lax.axis_index("ctx")
    member, plane = place % group, place // group
    head_place = lax.axis_index("head")

    def to_member(array, by):
        pairs = [(i, i // group * group + (i + by) % group) for i in range(context)]
        return lax.ppermute(array, "ctx", pairs)

    def between_planes(array, pairs):
        return lax.ppermute(
            array,
            "ctx",
            [(a * group + m, b * group + m) for a, b in pairs for m in range(group)],
        )

    def head_columns(array, by):
        return lax.dynamic_slice_in_dim(array, (member + by) % group * width, width, 1)

    gate, lift, down = (
        lax.dynamic_index_in_dim(w, member, 0, keepdims=False)
        for w in (fast_gate, fast_lift, fast_down)
    )
    gain = lax.dynamic_slice_in_dim(output_gain, member * width, width, 0)[None]

    keys, values, rates, asked = [], [], [], []
    for by in range(group):
        key_part, value_part = head_columns(key_rows, by), head_columns(value_rows, by)
        rate_part = lax.dynamic_index_in_dim(learning_rates, (member + by) % group, 0, keepdims=False)
        query_part = head_columns(queries, by)
        if by > 0:
            rate_part = to_member(rate_part, by)
            key_part = to_member(key_part, by)
            value_part = to_member(value_part, by)
            query_part = to_member(after(query_part, value_part), by)
        keys.append(key_part)
        values.append(value_part)
        rates.append(rate_part)
        asked.append(query_part)

    totals = None
    for by in range(group):
        parts = token_gradients(keys[by], values[by], rates[by], gate, lift, down)
        totals = parts if totals is None else tuple(a + b for a, b in zip(totals, parts))

    trees = (tree_low(0, planes), tree_high(0, planes), tree_mid(planes))
    owners = (0, planes - 1, planes // 2)
    rows = width // PIECES
    pieces = {}
    for piece in range(PIECES):
        for kind in range(3):
            pieces[kind, piece] = totals[kind][piece * rows : (piece + 1) * rows]
    for level in range(max(map(len, trees))):
        for piece in range(PIECES):
            for kind in range(3):
                if level < len(trees[kind]):
                    own = pieces[kind, piece]
                    pieces[kind, piece] = own + between_planes(own.astype(bf16), trees[kind][level]).astype(f32)
    sums = [jnp.concatenate([pieces[kind, piece] for piece in range(PIECES)]) for kind in range(3)]

    def by_owner(options):
        return jnp.where(
            plane == owners[0], options[0], jnp.where(plane == owners[1], options[1], options[2])
        )

    renewed = renew(by_owner(sums), by_owner((gate, lift, down)))

    ordered_keys = [pick(keys, (member - j) % group) for j in range(group)]
    ordered_values = [pick(values, (member - j) % group) for j in range(group)]
    ordered_queries = [pick(asked, (member - j) % group) for j in range(group)]
    onward = [(i, i + 1) for i in range(planes - 1)]
    earlier_keys = between_planes(ordered_keys[-1][-WINDOW:], onward)
    earlier_values = between_planes(ordered_values[-1][-WINDOW:], onward)
    attended = attention(
        jnp.concatenate(ordered_queries),
        earlier_keys,
        jnp.concatenate(ordered_keys),
        earlier_values,
        jnp.concatenate(ordered_values),
        plane,
    )

    held = {}
    for piece in range(PIECES):
        for kind in range(3):
            held[kind, piece] = renewed[piece * rows : (piece + 1) * rows]
    depth = max(map(len, trees))
    for level in reversed(range(depth)):
        for piece in range(PIECES):
            for kind in range(3):
                if level < len(trees[kind]):
                    pairs = [(b, a) for a, b in trees[kind][level]]
                    own = held[kind, piece]
                    got = between_planes(own, pairs)
                    here = functools.reduce(jnp.logical_or, [plane == b for _, b in pairs])
                    held[kind, piece] = jnp.where(here, got, own)
    new_gate, new_lift, new_down = (
        jnp.concatenate([held[kind, piece] for piece in range(PIECES)]) for kind in range(3)
    )

    chunks = []
    for by in list(range(1, group)) + [0]:
        owner = (member - by) % group
        combined = apply_fast(asked[by], new_gate, new_lift, new_down, attended, gain, owner)
        if by > 0:
            combined = to_member(combined, (group - by) % group)
        chunks.append((combined, (member + by) % group))
    chunks = chunks[-1:] + chunks[:-1]

    total = None
    for number, (chunk, head) in enumerate(chunks):
        parts, offsets = [chunk], [0]
        bit = columns_of // 2
        while bit:
            pairs = [(i, i ^ bit) for i in range(columns_of)]
            parts = parts + [lax.ppermute(part, "head", pairs) for part in parts]
            offsets = offsets + [o ^ bit for o in offsets]
            bit //= 2
        places = [(head_place ^ o) * group + head for o in offsets]
        total = project(parts, places, output_weight, total, number == len(chunks) - 1)
    return total


def solution(mesh):
    return jax.shard_map(
        on_device,
        mesh=mesh,
        in_specs=(
            P("ctx", "head"),
            P("ctx", "head"),
            P("ctx", "head"),
            P("head", "ctx"),
            P("head", None, None),
            P("head", None, None),
            P("head", None, None),
            P("head"),
            P(None, "head"),
        ),
        out_specs=P("ctx", "head"),
        check_vma=False,
    )
```

time: 414 us -> 278 us (0.67); the launches traced: 407 us -> 277 us
  matrix products: 127 us -> 15.6 us
  waiting for transfers between devices: 183 us -> 90.6 us
  starting transfers between devices: 10.3 us -> 88 us
  Pallas kernels: 0 us -> 55.6 us
  local copies, waits for them, and re-layouts: 35.4 us -> 11.5 us
  other arithmetic: 36.9 us -> 14.5 us
  between operations: 14.3 us -> 0.76 us
    psum x1 -> x0, waiting for transfers between devices: 124 us -> none  [on_device(): summed = lax.psum(partials.astype(jnp.bfloat16), 'ctx').astype(jnp.float32)]
    dot_general x19 -> x12, matrix products: 114 us -> 15.6 us  [mm(): return lax.dot_general(a, b, (dims, ((), ())), preferred_element_type=f32)]
    ppermute x2 -> x37, starting transfers between devices: 9.75 us -> 88 us  [the longest x26 82.2 us: between_planes(): lax.ppermute(array, 'ctx', [(a * group + m, b * group + m) for a, b in pa...]
    ppermute x2 -> x37, waiting for transfers between devices: 19.3 us -> 90.6 us  [the longest x26 62.4 us: between_planes(): lax.ppermute(array, 'ctx', [(a * group + m, b * group + m) for a, b in pa...]
    pallas_call x0 -> x6, Pallas kernels: none -> 55.6 us  [the longest x2 19.3 us: project(): pl.pallas_call(functools.partial(project_kernel, count, total is not None...]
    all_gather x1 -> x0, waiting for transfers between devices: 39.6 us -> none  [on_device(): lax.all_gather(combined, 'head', axis=1, tiled=True)]
    convert_element_type x5 -> x3, other arithmetic: 19.4 us -> 0.52 us  [on_device(): own.astype(bf16)]
    sub x1 -> x0, matrix products: 13.8 us -> none  [local_attention(): weights = jnp.exp(scores - row_peak)]
  transfers between devices with their start and end apart: 4 -> 37, of which waited for: 3 -> 16; matrix products, arithmetic and copies ran while one was open for 19% -> 12% of each run, Pallas kernels for 0% -> 15%
where the time goes in v1:
time: 278 us; the launch traced here: 277 us
  waiting for transfers between devices  90.6 us (33%)
  starting transfers between devices  88 us (32%)
  Pallas kernels  55.6 us (20%)
  matrix products  15.6 us (6%)
  other arithmetic  14.5 us (5%)
  local copies, waits for them, and re-layouts  11.5 us (4%)
    ppermute x26, starting transfers between devices, between_planes(): lax.ppermute(array, 'ctx', [(a * group + m, b * group + m) for a, b in pa...  82.2 us
    ppermute x26, waiting for transfers between devices, between_planes(): lax.ppermute(array, 'ctx', [(a * group + m, b * group + m) for a, b in pa...  62.4 us
    pallas_call x2, Pallas kernels, project(): pl.pallas_call(functools.partial(project_kernel, count, total is not None...  19.3 us
    ppermute x5, waiting for transfers between devices, to_member(): return lax.ppermute(array, 'ctx', pairs)  16.5 us
    dot_general x12, matrix products, mm(): return lax.dot_general(a, b, (dims, ((), ())), preferred_element_type=f32)  15.6 us
    pallas_call x1, Pallas kernels, attention(): pl.pallas_call(attention_kernel, out_shape=jax.ShapeDtypeStruct((tokens,...  15.4 us
    ppermute x6, waiting for transfers between devices, on_device(): parts = parts + [lax.ppermute(part, 'head', pairs) for part in parts]  11.7 us
    pallas_call x1, Pallas kernels, renew(): pl.pallas_call(settle_kernel, out_shape=jax.ShapeDtypeStruct((rows, colum...  10.6 us
  transfers between devices with their start and end apart: 37, of which 16 were waited for; matrix products, arithmetic and copies ran while one was open for 12% of the time, Pallas kernels for 15%

profile of v1, /device:TPU:0, one launch (start us, length us, event | category | flops | bytes accessed | tf_op | source)
XLA Modules:
  0.0 276.6 jit_solution(16402319717457504665)
XLA Ops:
  2.2 3.0 %collective-permute-start = (bf16[512,640]{1,0:T(8,128)(2,1)}, bf16[512,640]{1,0:T(8,128)(2,1)}, u32[]{:S(2)}, u32[]{:S(2)}) collective-permute-start(bf16[512,640]{1,0:T(8,128)(2,1)} %constant_dynamic-slice_fusion.4), channel_id=1, source_target_pairs={{0,4},{4,0},{8,12},{12,8},{16,20},{20,16},{24,28},{28,24},{1,5},{5... | collective-permute-start | bytes 1966088 | tf_op jit(solution)/shard_map/ppermute | solution.py:285
  24.1 10.9 %collective-permute-done.2 = bf16[512,640]{1,0:T(8,128)(2,1)S(1)} collective-permute-done((bf16[512,640]{1,0:T(8,128)(2,1)}, bf16[512,640]{1,0:T(8,128)(2,1)S(1)}, u32[]{:S(2)}, u32[]{:S(2)}) %collective-permute-start.2) | collective-permute-done | bytes 655392 | tf_op jit(solution)/shard_map/ppermute | solution.py:285
  43.8 4.7 %collective-permute-start.8 = (bf16[320,640]{1,0:T(8,128)(2,1)S(1)}, bf16[320,640]{1,0:T(8,128)(2,1)S(1)}, u32[]{:S(2)}, u32[]{:S(2)}) collective-permute-start(bf16[320,640]{1,0:T(8,128)(2,1)S(1)} %get-tuple-element.23), channel_id=1, source_target_pairs={{16,24},{20,28},{0,8},{4,12},{17,25},{21,29},{1,9},{5,13},{18,26},... | collective-permute-start | bytes 1228808 | tf_op jit(solution)/shard_map/ppermute | solution.py:288
  56.0 4.7 %collective-permute-done.6 = bf16[320,640]{1,0:T(8,128)(2,1)S(1)} collective-permute-done((bf16[320,640]{1,0:T(8,128)(2,1)S(1)}, bf16[320,640]{1,0:T(8,128)(2,1)S(1)}, u32[]{:S(2)}, u32[]{:S(2)}) %collective-permute-start.6) | collective-permute-done | bytes 409632 | tf_op jit(solution)/shard_map/ppermute | solution.py:288
  63.7 3.5 %collective-permute-done.10 = bf16[320,640]{1,0:T(8,128)(2,1)S(1)} collective-permute-done((bf16[320,640]{1,0:T(8,128)(2,1)S(1)}, bf16[320,640]{1,0:T(8,128)(2,1)S(1)}, u32[]{:S(2)}, u32[]{:S(2)}) %collective-permute-start.10) | collective-permute-done | bytes 409632 | tf_op jit(solution)/shard_map/ppermute | solution.py:288
  68.6 7.3 %collective-permute-done.12 = bf16[320,640]{1,0:T(8,128)(2,1)S(1)} collective-permute-done((bf16[320,640]{1,0:T(8,128)(2,1)S(1)}, bf16[320,640]{1,0:T(8,128)(2,1)S(1)}, u32[]{:S(2)}, u32[]{:S(2)}) %collective-permute-start.12) | collective-permute-done | bytes 409632 | tf_op jit(solution)/shard_map/ppermute | solution.py:288
  76.6 5.2 %collective-permute-done.14 = bf16[320,640]{1,0:T(8,128)(2,1)S(1)} collective-permute-done((bf16[320,640]{1,0:T(8,128)(2,1)S(1)}, bf16[320,640]{1,0:T(8,128)(2,1)S(1)}, u32[]{:S(2)}, u32[]{:S(2)}) %collective-permute-start.14) | collective-permute-done | bytes 409632 | tf_op jit(solution)/shard_map/ppermute | solution.py:288
  86.5 10.6 %shard_map.91 = bf16[640,640]{1,0:T(8,128)(2,1)} custom-call(f32[640,640]{1,0:T(8,128)} %maximum_select_fusion.grad_ref, bf16[640,640]{1,0:T(8,128)(2,1)} %bitcast_select_fusion.init_ref), custom_call_target="tpu_custom_call" | custom-call | flops 4718592000 | bytes 3276800 | tf_op jit(solution)/shard_map/pallas_call | solution.py:141
  100.6 31.2 %collective-permute-start.16 = (bf16[320,640]{1,0:T(8,128)(2,1)S(1)}, bf16[320,640]{1,0:T(8,128)(2,1)S(1)}, u32[]{:S(2)}, u32[]{:S(2)}) collective-permute-start(bf16[320,640]{1,0:T(8,128)(2,1)S(1)} %get-tuple-element.37), channel_id=1, source_target_pairs={{0,16},{4,20},{1,17},{5,21},{2,18},{6,22},{3,19},{7,23}} | collective-permute-start | bytes 1228808 | tf_op jit(solution)/shard_map/ppermute | solution.py:288
  137.3 4.4 %collective-permute-done.16 = bf16[320,640]{1,0:T(8,128)(2,1)S(1)} collective-permute-done((bf16[320,640]{1,0:T(8,128)(2,1)S(1)}, bf16[320,640]{1,0:T(8,128)(2,1)S(1)}, u32[]{:S(2)}, u32[]{:S(2)}) %collective-permute-start.16) | collective-permute-done | bytes 409632 | tf_op jit(solution)/shard_map/ppermute | solution.py:288
  141.7 11.5 %collective-permute-start.28 = (bf16[512,640]{1,0:T(8,128)(2,1)S(1)}, bf16[512,640]{1,0:T(8,128)(2,1)S(1)}, u32[]{:S(2)}, u32[]{:S(2)}) collective-permute-start(bf16[512,640]{1,0:T(8,128)(2,1)S(1)} %get-tuple-element.12), channel_id=1, source_target_pairs={{0,8},{4,12},{8,16},{12,20},{16,24},{20,28},{1,9},{5,13},{9,17},{1... | collective-permute-start | bytes 1966088 | tf_op jit(solution)/shard_map/ppermute | solution.py:288
  155.5 9.6 %collective-permute-start.19 = (bf16[320,640]{1,0:T(8,128)(2,1)S(1)}, bf16[320,640]{1,0:T(8,128)(2,1)S(1)}, u32[]{:S(2)}, u32[]{:S(2)}) collective-permute-start(bf16[320,640]{1,0:T(8,128)(2,1)S(1)} %get-tuple-element.33), channel_id=1, source_target_pairs={{0,8},{4,12},{16,24},{20,28},{1,9},{5,13},{17,25},{21,29},{2,10},{... | collective-permute-start | bytes 1228808 | tf_op jit(solution)/shard_map/ppermute | solution.py:288
  168.3 14.0 %collective-permute-done.29.vp_ref = bf16[512,640]{1,0:T(8,128)(2,1)S(1)} collective-permute-done((bf16[512,640]{1,0:T(8,128)(2,1)S(1)}, bf16[512,640]{1,0:T(8,128)(2,1)S(1)}, u32[]{:S(2)}, u32[]{:S(2)}) %collective-permute-start.29) | collective-permute-done | bytes 655392 | tf_op jit(solution)/shard_map/ppermute | solution.py:288
  183.3 15.4 %shard_map.92.att_ref = f32[1024,640]{1,0:T(8,128)} custom-call(s32[1]{0:T(128)} %bitcast.10.first_ref, bf16[1024,640]{1,0:T(8,128)(2,1)} %pad_maximum_fusion.q_ref, bf16[512,640]{1,0:T(8,128)(2,1)} %copy-done.21, bf16[1024,640]{1,0:T(8,128)(2,1)} %get-tuple-element.43.k_ref, bf16[512,640]{1,0:T(8,128)(2,1)} %copy-done.22, ...), custom_call_target="tpu_custom_call" | custom-call | flops 1677721600 | bytes 7864320 | tf_op jit(solution)/shard_map/pallas_call | solution.py:96
  204.2 8.7 %collective-permute-done.23 = bf16[320,640]{1,0:T(8,128)(2,1)S(1)} collective-permute-done((bf16[320,640]{1,0:T(8,128)(2,1)S(1)}, bf16[320,640]{1,0:T(8,128)(2,1)S(1)}, u32[]{:S(2)}, u32[]{:S(2)}) %collective-permute-start.23) | collective-permute-done | bytes 409632 | tf_op jit(solution)/shard_map/ppermute | solution.py:288
  213.0 4.4 %collective-permute-done.21 = bf16[320,640]{1,0:T(8,128)(2,1)S(1)} collective-permute-done((bf16[320,640]{1,0:T(8,128)(2,1)S(1)}, bf16[320,640]{1,0:T(8,128)(2,1)S(1)}, u32[]{:S(2)}, u32[]{:S(2)}) %collective-permute-start.21) | collective-permute-done | bytes 409632 | tf_op jit(solution)/shard_map/ppermute | solution.py:288
  221.8 4.3 %collective-permute-done.25 = bf16[320,640]{1,0:T(8,128)(2,1)S(1)} collective-permute-done((bf16[320,640]{1,0:T(8,128)(2,1)S(1)}, bf16[320,640]{1,0:T(8,128)(2,1)S(1)}, u32[]{:S(2)}, u32[]{:S(2)}) %collective-permute-start.25) | collective-permute-done | bytes 409632 | tf_op jit(solution)/shard_map/ppermute | solution.py:288
  227.2 5.2 %shard_map.93 = bf16[512,640]{1,0:T(8,128)(2,1)} custom-call(s32[1]{0:T(128)} %bitcast.4.which_ref, bf16[512,640]{1,0:T(8,128)(2,1)} %copy-done, bf16[640,640]{1,0:T(8,128)(2,1)} %pad_maximum_fusion.3.gate_ref, bf16[640,640]{1,0:T(8,128)(2,1)} %pad_maximum_fusion.4.lift_ref, bf16[640,640]{1,0:T(8,128)(2,1)} %pad_maximum_fusion.5.down_ref, ...), custom_call_target="tpu_custom_call" | custom-call | flops 1258291200 | bytes 5734400 | tf_op jit(solution)/shard_map/pallas_call | solution.py:169
  232.4 5.2 %shard_map.94.refs_1_ = bf16[512,640]{1,0:T(8,128)(2,1)} custom-call(s32[1]{0:T(128)} %bitcast.15.which_ref, bf16[512,640]{1,0:T(8,128)(2,1)} %copy-done.1, bf16[640,640]{1,0:T(8,128)(2,1)} %pad_maximum_fusion.3.gate_ref, bf16[640,640]{1,0:T(8,128)(2,1)} %pad_maximum_fusion.4.lift_ref, bf16[640,640]{1,0:T(8,128)(2,1)} %pad_maximum_fusion.5.down_ref, ...), custom_call_target="tpu_custom_call" | custom-call | flops 1258291200 | bytes 5734400 | tf_op jit(solution)/shard_map/pallas_call | solution.py:169
  237.5 5.6 %collective-permute-done.30.refs_1_ = bf16[512,640]{1,0:T(8,128)(2,1)S(1)} collective-permute-done((bf16[512,640]{1,0:T(8,128)(2,1)}, bf16[512,640]{1,0:T(8,128)(2,1)S(1)}, u32[]{:S(2)}, u32[]{:S(2)}) %collective-permute-start.30) | collective-permute-done | bytes 655392 | tf_op jit(solution)/shard_map/ppermute | solution.py:285
  243.2 5.2 %collective-permute-done.34.refs_2_ = bf16[512,640]{1,0:T(8,128)(2,1)S(1)} collective-permute-done((bf16[512,640]{1,0:T(8,128)(2,1)}, bf16[512,640]{1,0:T(8,128)(2,1)S(1)}, u32[]{:S(2)}, u32[]{:S(2)}) %collective-permute-start.34) | collective-permute-done | bytes 655392 | tf_op jit(solution)/shard_map/ppermute | solution.py:393
  248.9 6.5 %collective-permute-done.31.refs_2_ = bf16[512,640]{1,0:T(8,128)(2,1)S(1)} collective-permute-done((bf16[512,640]{1,0:T(8,128)(2,1)S(1)}, bf16[512,640]{1,0:T(8,128)(2,1)S(1)}, u32[]{:S(2)}, u32[]{:S(2)}) %collective-permute-start.31) | collective-permute-done | bytes 655392 | tf_op jit(solution)/shard_map/ppermute | solution.py:393
  256.2 9.4 %shard_map.95.refs_6_ = f32[512,1280]{1,0:T(8,128)} custom-call(s32[4]{0:T(128)} %get-tuple-element.42.refs_0_, bf16[512,640]{1,0:T(8,128)(2,1)} %shard_map.94.refs_1_, bf16[512,640]{1,0:T(8,128)(2,1)} %copy-done.23, bf16[512,640]{1,0:T(8,128)(2,1)} %collective-permute-done.35.refs_3_, bf16[512,640]{1,0:T(8,128)(2,1)} %collective-permute-done.36.refs_4_, ...), custom_call_target="tpu_custom_call" | custom-call | flops 3355443200 | bytes 14417920 | tf_op jit(solution)/shard_map/pallas_call | solution.py:226
  266.7 9.9 %shard_map.96 = bf16[512,1280]{1,0:T(8,128)(2,1)} custom-call(s32[4]{0:T(128)} %get-tuple-element.41.refs_0_, bf16[512,640]{1,0:T(8,128)(2,1)} %copy-done.17, bf16[512,640]{1,0:T(8,128)(2,1)} %copy-done.18, bf16[512,640]{1,0:T(8,128)(2,1)} %copy-done.19, bf16[512,640]{1,0:T(8,128)(2,1)} %copy-done.20, bf16[5120,1280]{1,0:T(8,128)(2,1)} %refs_5_.3, ...), custom_call_target="tpu_custom_call" | custom-call | flops 3355443200 | bytes 14417920 | tf_op jit(solution)/shard_map/pallas_call | solution.py:226
  (159 shorter events, 75.3 us)
Async XLA Ops:
  2.2 21.7 %collective-permute-start = (bf16[512,640]{1,0:T(8,128)(2,1)}, bf16[512,640]{1,0:T(8,128)(2,1)}, u32[]{:S(2)}, u32[]{:S(2)}) collective-permute-start(bf16[512,640]{1,0:T(8,128)(2,1)} %constant_dynamic-slice_fusion.4), channel_id=1, source_target_pairs={{0,4},{4,0},{8,12},{12,8},{16,20},{20,16},{24,28},{28,24},{1,5},{5... | collective-permute-start | bytes 1966088 | tf_op jit(solution)/shard_map/ppermute | solution.py:285
  6.0 28.9 %collective-permute-start.2 = (bf16[512,640]{1,0:T(8,128)(2,1)}, bf16[512,640]{1,0:T(8,128)(2,1)S(1)}, u32[]{:S(2)}, u32[]{:S(2)}) collective-permute-start(bf16[512,640]{1,0:T(8,128)(2,1)} %constant_dynamic-slice_fusion.2), channel_id=1, source_target_pairs={{0,4},{4,0},{8,12},{12,8},{16,20},{20,16},{24,28},{28,24},{1,5},{5... | collective-permute-start | bytes 1966088 | tf_op jit(solution)/shard_map/ppermute | solution.py:285
  6.0 30.5 %collective-permute-start.3 = (f32[512]{0:T(512)S(1)}, f32[512]{0:T(512)S(1)}, u32[]{:S(2)}, u32[]{:S(2)}) collective-permute-start(f32[512]{0:T(512)S(1)} %bitcast.39), channel_id=1, source_target_pairs={{0,4},{4,0},{8,12},{12,8},{16,20},{20,16},{24,28},{28,24},{1,5},{5... | collective-permute-start | bytes 6152 | tf_op jit(solution)/shard_map/ppermute | solution.py:285
  23.9 110.0 %collective-permute-start.1 = (bf16[512,640]{1,0:T(8,128)(2,1)}, bf16[512,640]{1,0:T(8,128)(2,1)S(1)}, u32[]{:S(2)}, u32[]{:S(2)}) collective-permute-start(bf16[512,640]{1,0:T(8,128)(2,1)} %constant_dynamic-slice_fusion.5), channel_id=1, source_target_pairs={{0,4},{4,0},{8,12},{12,8},{16,20},{20,16},{24,28},{28,24},{1,5},{5... | collective-permute-start | bytes 1966088 | tf_op jit(solution)/shard_map/ppermute | solution.py:285
  41.5 19.2 %collective-permute-start.6 = (bf16[320,640]{1,0:T(8,128)(2,1)S(1)}, bf16[320,640]{1,0:T(8,128)(2,1)S(1)}, u32[]{:S(2)}, u32[]{:S(2)}) collective-permute-start(bf16[320,640]{1,0:T(8,128)(2,1)S(1)} %get-tuple-element.30), channel_id=1, source_target_pairs={{8,0},{12,4},{24,16},{28,20},{9,1},{13,5},{25,17},{29,21},{10,2},{... | collective-permute-start | bytes 1228808 | tf_op jit(solution)/shard_map/ppermute | solution.py:288
  43.8 18.6 %collective-permute-start.8 = (bf16[320,640]{1,0:T(8,128)(2,1)S(1)}, bf16[320,640]{1,0:T(8,128)(2,1)S(1)}, u32[]{:S(2)}, u32[]{:S(2)}) collective-permute-start(bf16[320,640]{1,0:T(8,128)(2,1)S(1)} %get-tuple-element.23), channel_id=1, source_target_pairs={{16,24},{20,28},{0,8},{4,12},{17,25},{21,29},{1,9},{5,13},{18,26},... | collective-permute-start | bytes 1228808 | tf_op jit(solution)/shard_map/ppermute | solution.py:288
  48.5 18.7 %collective-permute-start.10 = (bf16[320,640]{1,0:T(8,128)(2,1)S(1)}, bf16[320,640]{1,0:T(8,128)(2,1)S(1)}, u32[]{:S(2)}, u32[]{:S(2)}) collective-permute-start(bf16[320,640]{1,0:T(8,128)(2,1)S(1)} %get-tuple-element.24), channel_id=1, source_target_pairs={{16,24},{20,28},{0,8},{4,12},{17,25},{21,29},{1,9},{5,13},{18,26},... | collective-permute-start | bytes 1228808 | tf_op jit(solution)/shard_map/ppermute | solution.py:288
  54.5 21.4 %collective-permute-start.12 = (bf16[320,640]{1,0:T(8,128)(2,1)S(1)}, bf16[320,640]{1,0:T(8,128)(2,1)S(1)}, u32[]{:S(2)}, u32[]{:S(2)}) collective-permute-start(bf16[320,640]{1,0:T(8,128)(2,1)S(1)} %get-tuple-element.17), channel_id=1, source_target_pairs={{0,8},{4,12},{24,16},{28,20},{1,9},{5,13},{25,17},{29,21},{2,10},{... | collective-permute-start | bytes 1228808 | tf_op jit(solution)/shard_map/ppermute | solution.py:288
  60.7 21.2 %collective-permute-start.14 = (bf16[320,640]{1,0:T(8,128)(2,1)S(1)}, bf16[320,640]{1,0:T(8,128)(2,1)S(1)}, u32[]{:S(2)}, u32[]{:S(2)}) collective-permute-start(bf16[320,640]{1,0:T(8,128)(2,1)S(1)} %get-tuple-element.18), channel_id=1, source_target_pairs={{0,8},{4,12},{24,16},{28,20},{1,9},{5,13},{25,17},{29,21},{2,10},{... | collective-permute-start | bytes 1228808 | tf_op jit(solution)/shard_map/ppermute | solution.py:288
  62.4 20.4 %collective-permute-start.5 = (bf16[320,640]{1,0:T(8,128)(2,1)S(1)}, bf16[320,640]{1,0:T(8,128)(2,1)S(1)}, u32[]{:S(2)}, u32[]{:S(2)}) collective-permute-start(bf16[320,640]{1,0:T(8,128)(2,1)S(1)} %get-tuple-element.27), channel_id=1, source_target_pairs={{16,0},{20,4},{17,1},{21,5},{18,2},{22,6},{19,3},{23,7}} | collective-permute-start | bytes 1228808 | tf_op jit(solution)/shard_map/ppermute | solution.py:288
  98.3 36.3 %collective-permute-start.24 = (bf16[320,640]{1,0:T(8,128)(2,1)S(1)}, bf16[320,640]{1,0:T(8,128)(2,1)S(1)}, u32[]{:S(2)}, u32[]{:S(2)}) collective-permute-start(bf16[320,640]{1,0:T(8,128)(2,1)S(1)} %get-tuple-element.37), channel_id=1, source_target_pairs={{16,8},{20,12},{17,9},{21,13},{18,10},{22,14},{19,11},{23,15}} | collective-permute-start | bytes 1228808 | tf_op jit(solution)/shard_map/ppermute | solution.py:288
  100.6 41.1 %collective-permute-start.16 = (bf16[320,640]{1,0:T(8,128)(2,1)S(1)}, bf16[320,640]{1,0:T(8,128)(2,1)S(1)}, u32[]{:S(2)}, u32[]{:S(2)}) collective-permute-start(bf16[320,640]{1,0:T(8,128)(2,1)S(1)} %get-tuple-element.37), channel_id=1, source_target_pairs={{0,16},{4,20},{1,17},{5,21},{2,18},{6,22},{3,19},{7,23}} | collective-permute-start | bytes 1228808 | tf_op jit(solution)/shard_map/ppermute | solution.py:288
  131.9 21.4 %collective-permute-start.18 = (bf16[320,640]{1,0:T(8,128)(2,1)S(1)}, bf16[320,640]{1,0:T(8,128)(2,1)S(1)}, u32[]{:S(2)}, u32[]{:S(2)}) collective-permute-start(bf16[320,640]{1,0:T(8,128)(2,1)S(1)} %get-tuple-element.38), channel_id=1, source_target_pairs={{0,16},{4,20},{1,17},{5,21},{2,18},{6,22},{3,19},{7,23}} | collective-permute-start | bytes 1228808 | tf_op jit(solution)/shard_map/ppermute | solution.py:288
  133.2 22.0 %collective-permute-start.22 = (bf16[320,640]{1,0:T(8,128)(2,1)S(1)}, bf16[320,640]{1,0:T(8,128)(2,1)S(1)}, u32[]{:S(2)}, u32[]{:S(2)}) collective-permute-start(bf16[320,640]{1,0:T(8,128)(2,1)S(1)} %get-tuple-element.38), channel_id=1, source_target_pairs={{24,8},{28,12},{25,9},{29,13},{26,10},{30,14},{27,11},{31,15}} | collective-permute-start | bytes 1228808 | tf_op jit(solution)/shard_map/ppermute | solution.py:288
  133.9 21.3 %collective-permute-start.26 = (bf16[320,640]{1,0:T(8,128)(2,1)S(1)}, bf16[320,640]{1,0:T(8,128)(2,1)S(1)}, u32[]{:S(2)}, u32[]{:S(2)}) collective-permute-start(bf16[320,640]{1,0:T(8,128)(2,1)S(1)} %get-tuple-element.38), channel_id=1, source_target_pairs={{16,8},{20,12},{17,9},{21,13},{18,10},{22,14},{19,11},{23,15}} | collective-permute-start | bytes 1228808 | tf_op jit(solution)/shard_map/ppermute | solution.py:288
  134.6 20.6 %collective-permute-start.20 = (bf16[320,640]{1,0:T(8,128)(2,1)S(1)}, bf16[320,640]{1,0:T(8,128)(2,1)S(1)}, u32[]{:S(2)}, u32[]{:S(2)}) collective-permute-start(bf16[320,640]{1,0:T(8,128)(2,1)S(1)} %get-tuple-element.37), channel_id=1, source_target_pairs={{24,8},{28,12},{25,9},{29,13},{26,10},{30,14},{27,11},{31,15}} | collective-permute-start | bytes 1228808 | tf_op jit(solution)/shard_map/ppermute | solution.py:288
  141.7 26.6 %collective-permute-start.28 = (bf16[512,640]{1,0:T(8,128)(2,1)S(1)}, bf16[512,640]{1,0:T(8,128)(2,1)S(1)}, u32[]{:S(2)}, u32[]{:S(2)}) collective-permute-start(bf16[512,640]{1,0:T(8,128)(2,1)S(1)} %get-tuple-element.12), channel_id=1, source_target_pairs={{0,8},{4,12},{8,16},{12,20},{16,24},{20,28},{1,9},{5,13},{9,17},{1... | collective-permute-start | bytes 1966088 | tf_op jit(solution)/shard_map/ppermute | solution.py:288
  153.2 29.2 %collective-permute-start.29 = (bf16[512,640]{1,0:T(8,128)(2,1)S(1)}, bf16[512,640]{1,0:T(8,128)(2,1)S(1)}, u32[]{:S(2)}, u32[]{:S(2)}) collective-permute-start(bf16[512,640]{1,0:T(8,128)(2,1)S(1)} %get-tuple-element.10), channel_id=1, source_target_pairs={{0,8},{4,12},{8,16},{12,20},{16,24},{20,28},{1,9},{5,13},{9,17},{1... | collective-permute-start | bytes 1966088 | tf_op jit(solution)/shard_map/ppermute | solution.py:288
  155.5 47.1 %collective-permute-start.19 = (bf16[320,640]{1,0:T(8,128)(2,1)S(1)}, bf16[320,640]{1,0:T(8,128)(2,1)S(1)}, u32[]{:S(2)}, u32[]{:S(2)}) collective-permute-start(bf16[320,640]{1,0:T(8,128)(2,1)S(1)} %get-tuple-element.33), channel_id=1, source_target_pairs={{0,8},{4,12},{16,24},{20,28},{1,9},{5,13},{17,25},{21,29},{2,10},{... | collective-permute-start | bytes 1228808 | tf_op jit(solution)/shard_map/ppermute | solution.py:288
  166.4 37.8 %collective-permute-start.17 = (bf16[320,640]{1,0:T(8,128)(2,1)S(1)}, bf16[320,640]{1,0:T(8,128)(2,1)S(1)}, u32[]{:S(2)}, u32[]{:S(2)}) collective-permute-start(bf16[320,640]{1,0:T(8,128)(2,1)S(1)} %get-tuple-element.32), channel_id=1, source_target_pairs={{0,8},{4,12},{16,24},{20,28},{1,9},{5,13},{17,25},{21,29},{2,10},{... | collective-permute-start | bytes 1228808 | tf_op jit(solution)/shard_map/ppermute | solution.py:288
  199.9 17.4 %collective-permute-start.21 = (bf16[320,640]{1,0:T(8,128)(2,1)S(1)}, bf16[320,640]{1,0:T(8,128)(2,1)S(1)}, u32[]{:S(2)}, u32[]{:S(2)}) collective-permute-start(bf16[320,640]{1,0:T(8,128)(2,1)S(1)} %get-tuple-element.36), channel_id=1, source_target_pairs={{24,16},{28,20},{8,0},{12,4},{25,17},{29,21},{9,1},{13,5},{26,18},... | collective-permute-start | bytes 1228808 | tf_op jit(solution)/shard_map/ppermute | solution.py:288
  201.2 20.5 %collective-permute-start.27 = (bf16[320,640]{1,0:T(8,128)(2,1)S(1)}, bf16[320,640]{1,0:T(8,128)(2,1)S(1)}, u32[]{:S(2)}, u32[]{:S(2)}) collective-permute-start(bf16[320,640]{1,0:T(8,128)(2,1)S(1)} %get-tuple-element.35), channel_id=1, source_target_pairs={{8,0},{12,4},{16,24},{20,28},{9,1},{13,5},{17,25},{21,29},{10,2},{... | collective-permute-start | bytes 1228808 | tf_op jit(solution)/shard_map/ppermute | solution.py:288
  202.6 23.6 %collective-permute-start.25 = (bf16[320,640]{1,0:T(8,128)(2,1)S(1)}, bf16[320,640]{1,0:T(8,128)(2,1)S(1)}, u32[]{:S(2)}, u32[]{:S(2)}) collective-permute-start(bf16[320,640]{1,0:T(8,128)(2,1)S(1)} %get-tuple-element.31), channel_id=1, source_target_pairs={{8,0},{12,4},{16,24},{20,28},{9,1},{13,5},{17,25},{21,29},{10,2},{... | collective-permute-start | bytes 1228808 | tf_op jit(solution)/shard_map/ppermute | solution.py:288
  248.4 17.2 %collective-permute-start.32 = (bf16[512,640]{1,0:T(8,128)(2,1)S(1)}, bf16[512,640]{1,0:T(8,128)(2,1)S(1)}, u32[]{:S(2)}, u32[]{:S(2)}) collective-permute-start(bf16[512,640]{1,0:T(8,128)(2,1)S(1)} %collective-permute-done.30.refs_1_), channel_id=1, source_target_pairs={{0,1},{1,0},{2,3},{3,2},{4,5},{5,4},{6,7},{7,6},{8,9},{9,8},{10,11... | collective-permute-start | bytes 1966088 | tf_op jit(solution)/shard_map/ppermute | solution.py:393
  (41 other events, 337.9 us)

commit v2 on v1

--- a/solution.py
+++ b/solution.py
@@ -12,7 +12,7 @@
 WINDOW = 512
 NS_ITERS = 3
 PIECES = 2
-VMEM_BYTES = 56 * 1024 * 1024
+VMEM_BYTES = 24 * 1024 * 1024
 
 quintic_first = 3.4445
 quintic_second = -4.775
@@ -54,6 +54,15 @@
     ]
 
 
+def tree_far(count):
+    levels, size = [], count
+    while size > 1:
+        half = (size + 1) // 2
+        levels.append([(i + half, i) for i in range(size - half)])
+        size = half
+    return levels
+
+
 def tree_mid(count):
     middle = count // 2
     left, right = tree_high(0, middle), tree_low(middle, count)
@@ -61,6 +70,12 @@
     for k in range(max(len(left), len(right))):
         levels.append((left[k] if k < len(left) else []) + (right[k] if k < len(right) else []))
     return levels + [[(middle - 1, middle)]]
+
+
+def spread_halves(count):
+    half = count // 2
+    low = [[(b, a) for a, b in level] for level in reversed(tree_low(0, half))]
+    return [level + [(count - 1 - a, count - 1 - b) for a, b in level] for level in low]
 
 
 def attention_kernel(first_ref, q_ref, kp_ref, k_ref, vp_ref, v_ref, out_ref, k_all, v_all):
@@ -112,35 +127,44 @@
     )(jnp.reshape(plane, (1,)).astype(jnp.int32), q, kp, k, vp, v)
 
 
-def settle_kernel(grad_ref, init_ref, out_ref, x_ref):
-    g = grad_ref[...]
-    square = jnp.sum(jnp.sum(g * g, axis=0, keepdims=True), axis=1, keepdims=True)
-    x_ref[...] = (g / (jnp.sqrt(square) + 1e-06)).astype(bf16)
-
-    @pl.loop(0, NS_ITERS)
-    def _(_):
-        x = x_ref[...]
-        gram = mm(x, x, ((1,), (1,))).astype(bf16)
-        product = mm(gram, x).astype(bf16)
-        second = mm(gram, product)
-        x_ref[...] = (
-            quintic_first * x.astype(f32)
-            + quintic_second * product.astype(f32)
-            + quintic_third * second
-        ).astype(bf16)
-
-    initial = init_ref[...].astype(f32)
-    updated = initial + x_ref[...].astype(f32)
-    target = jnp.sqrt(jnp.sum(initial * initial, axis=0, keepdims=True))
-    current = jnp.sqrt(jnp.sum(updated * updated, axis=0, keepdims=True) + 1e-06)
-    out_ref[...] = (updated * (target / current)).astype(bf16)
-
-
-def renew(gradient, initial):
+def settle_kernel(active_ref, grad_ref, init_ref, out_ref, x_ref):
+    @pl.when(active_ref[0] == 1)
+    def _():
+        g = grad_ref[...]
+        square = jnp.sum(jnp.sum(g * g, axis=0, keepdims=True), axis=1, keepdims=True)
+        x_ref[...] = (g / (jnp.sqrt(square) + 1e-06)).astype(bf16)
+
+        @pl.loop(0, NS_ITERS)
+        def _(_):
+            x = x_ref[...]
+            gram = mm(x, x, ((1,), (1,))).astype(bf16)
+            product = mm(gram, x).astype(bf16)
+            second = mm(gram, product)
+            x_ref[...] = (
+                quintic_first * x.astype(f32)
+                + quintic_second * product.astype(f32)
+                + quintic_third * second
+            ).astype(bf16)
+
+        initial = init_ref[...].astype(f32)
+        updated = initial + x_ref[...].astype(f32)
+        target = jnp.sqrt(jnp.sum(initial * initial, axis=0, keepdims=True))
+        current = jnp.sqrt(jnp.sum(updated * updated, axis=0, keepdims=True) + 1e-06)
+        out_ref[...] = (updated * (target / current)).astype(bf16)
+
+    @pl.when(active_ref[0] == 0)
+    def _():
+        out_ref[...] = jnp.zeros_like(out_ref)
+
+
+def renew(gradient, initial, active):
     rows, columns = gradient.shape
+    vmem = pl.BlockSpec(memory_space=pltpu.VMEM)
     return pl.pallas_call(
         settle_kernel,
         out_shape=jax.ShapeDtypeStruct((rows, columns), bf16),
+        in_specs=[pl.BlockSpec(memory_space=pltpu.SMEM), vmem, vmem],
+        out_specs=vmem,
         scratch_shapes=[pltpu.VMEM((rows, columns), bf16)],
         compiler_params=pltpu.CompilerParams(vmem_limit_bytes=VMEM_BYTES),
         cost_estimate=pl.CostEstimate(
@@ -148,7 +172,7 @@
             bytes_accessed=8 * rows * columns,
             transcendentals=0,
         ),
-    )(gradient, initial)
+    )(jnp.reshape(active, (1,)).astype(jnp.int32), gradient, initial)
 
 
 def apply_kernel(which_ref, q_ref, gate_ref, lift_ref, down_ref, att_ref, gain_ref, out_ref):
@@ -242,22 +266,16 @@
     )(jnp.stack(places).astype(jnp.int32), *operands)
 
 
-def token_gradients(keys, values, rates, gate, lift, down):
+OVER_TOKENS = ((0,), (0,))
+
+
+def forward(keys, gate, lift):
     gate_pre = mm(keys, gate)
     lift_pre = mm(keys, lift)
     logistic = jax.nn.sigmoid(gate_pre)
     silu = gate_pre * logistic
     hidden = (silu * lift_pre).astype(bf16)
-    scaled = (rates[:, None] * values.astype(f32)).astype(bf16)
-    backward = mm(scaled, down, ((1,), (1,)))
-    grad_gate = (backward * lift_pre * (logistic * (1.0 + gate_pre * (1.0 - logistic)))).astype(bf16)
-    grad_lift = (backward * silu).astype(bf16)
-    over_tokens = ((0,), (0,))
-    return (
-        mm(keys, grad_gate, over_tokens),
-        mm(keys, grad_lift, over_tokens),
-        mm(hidden, scaled, over_tokens),
-    )
+    return hidden, lift_pre * (logistic * (1.0 + gate_pre * (1.0 - logistic))), silu
 
 
 def on_device(
@@ -300,56 +318,110 @@
     )
     gain = lax.dynamic_slice_in_dim(output_gain, member * width, width, 0)[None]
 
-    keys, values, rates, asked = [], [], [], []
+    onward = [(i, i + 1) for i in range(planes - 1)]
+
+    def in_order(blocks):
+        return [pick(blocks, (member - j) % group) for j in range(group)]
+
+    keys = [head_columns(key_rows, by) for by in range(group)]
+    values = [head_columns(value_rows, by) for by in range(group)]
+    asked = [head_columns(queries, by) for by in range(group)]
+    rates = [
+        lax.dynamic_index_in_dim(learning_rates, (member + by) % group, 0, keepdims=False)
+        for by in range(group)
+    ]
+    keys = keys[:1] + [to_member(keys[by], by) for by in range(1, group)]
+    rates = rates[:1] + [to_member(rates[by], by) for by in range(1, group)]
+    values = values[:1] + [to_member(values[by], by) for by in range(1, group)]
+    asked = asked[:1] + [to_member(after(asked[by], values[-1]), by) for by in range(1, group)]
+    ordered_keys, ordered_values = in_order(keys), in_order(values)
+    earlier_keys = between_planes(ordered_keys[-1][-WINDOW:], onward)
+
+    hiddens, slopes, silus, scaleds = [], [], [], []
+    total_down = 0.0
     for by in range(group):
-        key_part, value_part = head_columns(key_rows, by), head_columns(value_rows, by)
-        rate_part = lax.dynamic_index_in_dim(learning_rates, (member + by) % group, 0, keepdims=False)
-        query_part = head_columns(queries, by)
-        if by > 0:
-            rate_part = to_member(rate_part, by)
-            key_part = to_member(key_part, by)
-            value_part = to_member(value_part, by)
-            query_part = to_member(after(query_part, value_part), by)
-        keys.append(key_part)
-        values.append(value_part)
-        rates.append(rate_part)
-        asked.append(query_part)
-
-    totals = None
+        hidden, slope, silu = forward(keys[by], gate, lift)
+        scaled = (rates[by][:, None] * after(values[by], hidden, earlier_keys).astype(f32)).astype(bf16)
+        total_down = total_down + mm(hidden, scaled, OVER_TOKENS)
+        slopes.append(slope)
+        silus.append(silu)
+        scaleds.append(scaled)
+    total_gate, total_lift = 0.0, 0.0
     for by in range(group):
-        parts = token_gradients(keys[by], values[by], rates[by], gate, lift, down)
-        totals = parts if totals is None else tuple(a + b for a, b in zip(totals, parts))
-
-    trees = (tree_low(0, planes), tree_high(0, planes), tree_mid(planes))
-    owners = (0, planes - 1, planes // 2)
+        scaled = scaleds[by] if by < group - 1 else after(scaleds[by], total_down)
+        backward = mm(scaled, down, ((1,), (1,)))
+        total_gate = total_gate + mm(keys[by], (backward * slopes[by]).astype(bf16), OVER_TOKENS)
+        total_lift = total_lift + mm(keys[by], (backward * silus[by]).astype(bf16), OVER_TOKENS)
+
     rows = width // PIECES
-    pieces = {}
-    for piece in range(PIECES):
-        for kind in range(3):
-            pieces[kind, piece] = totals[kind][piece * rows : (piece + 1) * rows]
-    for level in range(max(map(len, trees))):
-        for piece in range(PIECES):
-            for kind in range(3):
-                if level < len(trees[kind]):
-                    own = pieces[kind, piece]
-                    pieces[kind, piece] = own + between_planes(own.astype(bf16), trees[kind][level]).astype(f32)
-    sums = [jnp.concatenate([pieces[kind, piece] for piece in range(PIECES)]) for kind in range(3)]
-
-    def by_owner(options):
-        return jnp.where(
-            plane == owners[0], options[0], jnp.where(plane == owners[1], options[1], options[2])
-        )
-
-    renewed = renew(by_owner(sums), by_owner((gate, lift, down)))
-
-    ordered_keys = [pick(keys, (member - j) % group) for j in range(group)]
-    ordered_values = [pick(values, (member - j) % group) for j in range(group)]
-    ordered_queries = [pick(asked, (member - j) % group) for j in range(group)]
-    onward = [(i, i + 1) for i in range(planes - 1)]
-    earlier_keys = between_planes(ordered_keys[-1][-WINDOW:], onward)
-    earlier_values = between_planes(ordered_values[-1][-WINDOW:], onward)
+
+    def cut(matrix):
+        return [matrix[piece * rows : (piece + 1) * rows] for piece in range(PIECES)]
+
+    def summed(pieces, level):
+        return [own + between_planes(own.astype(bf16), level).astype(f32) for own in pieces]
+
+    gate_tree, lift_tree, down_tree = tree_far(planes), tree_high(0, planes), tree_mid(planes)
+    down_pieces = summed(cut(total_down), down_tree[0])
+    gate_pieces, lift_pieces = [], []
+    for piece, (a, b) in enumerate(zip(cut(total_gate), cut(total_lift))):
+        before = down_pieces[:1] if piece == 0 else down_pieces[1:] + asked[-1:]
+        gate_pieces += summed([after(a, *before)], gate_tree[0])
+        lift_pieces += summed([after(b, *before)], lift_tree[0])
+    for level in down_tree[1:]:
+        down_pieces = summed(down_pieces, level)
+    met = gate_pieces[:1] + lift_pieces[:1]
+    for level in range(1, len(gate_tree)):
+        gate_pieces = summed(gate_pieces, gate_tree[level])
+        lift_pieces = summed(lift_pieces, lift_tree[level])
+
+    middle_plane = plane == planes // 2
+    new_down = renew(after(jnp.concatenate(down_pieces), *met), down, middle_plane)
+
+    def spread(own, pairs):
+        got = between_planes(own, pairs)
+        here = functools.reduce(jnp.logical_or, [plane == b for _, b in pairs])
+        return jnp.where(here, got, own)
+
+    down_levels = [[(b, a) for a, b in level] for level in reversed(down_tree)]
+    down_pieces = [spread(own, down_levels[0]) for own in cut(new_down)]
+
+    low_plane, high_plane = plane == 0, plane == planes - 1
+    new_sums = jnp.concatenate(
+        [jnp.where(low_plane, a, b) for a, b in zip(gate_pieces, lift_pieces)]
+    )
+    earlier_values = between_planes(after(ordered_values[-1][-WINDOW:], new_sums), onward)
+    new_outer = renew(
+        after(new_sums, down_pieces[0]),
+        jnp.where(low_plane, gate, lift),
+        low_plane | high_plane,
+    )
+    for level in down_levels[1:]:
+        down_pieces = [spread(own, level) for own in down_pieces]
+    half = planes // 2
+    swap = [(i, (i + half) % planes) for i in range(planes)]
+    owners = [pair for pair in swap if pair[0] in (0, planes - 1)]
+    others = [pair for pair in swap if pair not in owners]
+    is_owner_swap = functools.reduce(jnp.logical_or, [plane == b for _, b in owners])
+    near, far = [], []
+    for piece, own in enumerate(cut(new_outer)):
+        own = own if piece == 0 else after(own, earlier_values)
+        far_own = between_planes(own, owners)
+        for level in spread_halves(planes):
+            own = spread(own, level)
+        near.append(own)
+        far.append(far_own)
+    far = [
+        jnp.where(is_owner_swap, first, between_planes(own, others))
+        for own, first in zip(near, far)
+    ]
+    lower = plane < half
+    new_gate = jnp.concatenate([jnp.where(lower, a, b) for a, b in zip(near, far)])
+    new_lift = jnp.concatenate([jnp.where(lower, b, a) for a, b in zip(near, far)])
+    new_down = jnp.concatenate(down_pieces)
+
     attended = attention(
-        jnp.concatenate(ordered_queries),
+        after(jnp.concatenate(in_order(asked)), *near),
         earlier_keys,
         jnp.concatenate(ordered_keys),
         earlier_values,
@@ -357,31 +429,13 @@
         plane,
     )
 
-    held = {}
-    for piece in range(PIECES):
-        for kind in range(3):
-            held[kind, piece] = renewed[piece * rows : (piece + 1) * rows]
-    depth = max(map(len, trees))
-    for level in reversed(range(depth)):
-        for piece in range(PIECES):
-            for kind in range(3):
-                if level < len(trees[kind]):
-                    pairs = [(b, a) for a, b in trees[kind][level]]
-                    own = held[kind, piece]
-                    got = between_planes(own, pairs)
-                    here = functools.reduce(jnp.logical_or, [plane == b for _, b in pairs])
-                    held[kind, piece] = jnp.where(here, got, own)
-    new_gate, new_lift, new_down = (
-        jnp.concatenate([held[kind, piece] for piece in range(PIECES)]) for kind in range(3)
-    )
-
-    chunks = []
+    chunks, combined = [], None
     for by in list(range(1, group)) + [0]:
         owner = (member - by) % group
-        combined = apply_fast(asked[by], new_gate, new_lift, new_down, attended, gain, owner)
-        if by > 0:
-            combined = to_member(combined, (group - by) % group)
-        chunks.append((combined, (member + by) % group))
+        wanted = asked[by] if combined is None else after(asked[by], combined)
+        combined = apply_fast(wanted, new_gate, new_lift, new_down, attended, gain, owner)
+        chunk = to_member(combined, group - by) if by > 0 else combined
+        chunks.append((chunk, (member + by) % group))
     chunks = chunks[-1:] + chunks[:-1]
 
     total = None
@@ -390,7 +444,10 @@
         bit = columns_of // 2
         while bit:
             pairs = [(i, i ^ bit) for i in range(columns_of)]
-            parts = parts + [lax.ppermute(part, "head", pairs) for part in parts]
+            parts = parts + [
+                after(lax.ppermute(part, "head", pairs), *([] if total is None else [total]))
+                for part in parts
+            ]
             offsets = offsets + [o ^ bit for o in offsets]
             bit //= 2
         places = [(head_place ^ o) * group + head for o in offsets]

time: 278 us -> 238 us (0.86)
  starting transfers between devices: 88 us -> 66.2 us
  Pallas kernels: 55.6 us -> 40.9 us
  local copies, waits for them, and re-layouts: 11.5 us -> 25.4 us
  waiting for transfers between devices: 90.6 us -> 79.2 us
  other arithmetic: 14.5 us -> 6.32 us
    ppermute x26 -> x24, starting transfers between devices: 82.2 us -> 56.7 us  [between_planes(): lax.ppermute(array, 'ctx', [(a * group + m, b * group + m) for a, b in pa...]
    unnamed x56 -> x44, local copies, waits for them, and re-layouts: 4.29 us -> 20.9 us
    ppermute x26 -> x24, waiting for transfers between devices: 62.4 us -> 55 us  [between_planes(): lax.ppermute(array, 'ctx', [(a * group + m, b * group + m) for a, b in pa...]
    pallas_call x2, Pallas kernels: 19.3 us -> 13.5 us  [project(): pl.pallas_call(functools.partial(project_kernel, count, total is not None...]
    pallas_call x2, Pallas kernels: 10.3 us -> 5.03 us  [apply_fast(): pl.pallas_call(apply_kernel, out_shape=jax.ShapeDtypeStruct((tokens, widt...]
    ppermute x5, waiting for transfers between devices: 16.5 us -> 12.4 us  [to_member(): return lax.ppermute(array, 'ctx', pairs)]
    concatenate x4 -> x6, other arithmetic: 4.08 us -> 0.66 us  [the longest x1 0.14 us: on_device(): jnp.concatenate([jnp.where(lower, a, b) for a, b in zip(near, far)])]
    pallas_call x1 -> x2, Pallas kernels: 10.6 us -> 8.14 us  [renew(): pl.pallas_call(settle_kernel, out_shape=jax.ShapeDtypeStruct((rows, colum...]
  transfers between devices with their start and end apart: 37 -> 35, of which waited for: 16 -> 15; matrix products, arithmetic and copies ran while one was open for 12% -> 11% of each run, Pallas kernels for 15% -> 12%
where the time goes in v2:
time: 238 us; the launch traced here: 237 us
  waiting for transfers between devices  79.2 us (33%)
  starting transfers between devices  66.2 us (28%)
  Pallas kernels  40.9 us (17%)
  local copies, waits for them, and re-layouts  25.4 us (11%)
  matrix products  18.3 us (8%)
  other arithmetic  6.32 us (3%)
    ppermute x24, starting transfers between devices, between_planes(): lax.ppermute(array, 'ctx', [(a * group + m, b * group + m) for a, b in pa...  56.7 us
    ppermute x24, waiting for transfers between devices, between_planes(): lax.ppermute(array, 'ctx', [(a * group + m, b * group + m) for a, b in pa...  55 us
    unnamed x44, local copies, waits for them, and re-layouts  20.9 us
    dot_general x12, matrix products, mm(): return lax.dot_general(a, b, (dims, ((), ())), preferred_element_type=f32)  18.3 us
    pallas_call x1, Pallas kernels, attention(): pl.pallas_call(attention_kernel, out_shape=jax.ShapeDtypeStruct((tokens,...  14.2 us
    pallas_call x2, Pallas kernels, project(): pl.pallas_call(functools.partial(project_kernel, count, total is not None...  13.5 us
    ppermute x5, waiting for transfers between devices, to_member(): return lax.ppermute(array, 'ctx', pairs)  12.4 us
    ppermute x6, waiting for transfers between devices, on_device(): lax.ppermute(part, 'head', pairs)  11.8 us
  transfers between devices with their start and end apart: 35, of which 15 were waited for; matrix products, arithmetic and copies ran while one was open for 11% of the time, Pallas kernels for 12%

profile of v2, /device:TPU:0, one launch (start us, length us, event | category | flops | bytes accessed | tf_op | source)
XLA Modules:
  0.0 237.1 jit_solution(15803139116187241561)
XLA Ops:
  10.8 3.3 %fusion.8 = f32[512,640]{1,0:T(8,128)} fusion(bf16[2,640,640]{2,1,0:T(8,128)(2,1)} %param.13, s32[]{:T(128)S(6)} %select_n.198, bf16[512,1280]{1,0:T(8,128)(2,1)} %param.10, s32[]{:T(128)S(6)} %select_n.196), kind=kOutput, calls=%fused_computation.30 | convolution fusion | flops 419430400 | bytes 2785288 | tf_op jit(solution)/shard_map/dot_general | solution.py:26
  17.7 3.3 %collective-permute-done.2 = bf16[512,640]{1,0:T(8,128)(2,1)} collective-permute-done((bf16[512,640]{1,0:T(8,128)(2,1)}, bf16[512,640]{1,0:T(8,128)(2,1)}, u32[]{:S(2)}, u32[]{:S(2)}) %collective-permute-start.2) | collective-permute-done | bytes 655392 | tf_op jit(solution)/shard_map/ppermute | solution.py:303
  22.3 4.1 %collective-permute-start.3 = (bf16[512,640]{1,0:T(8,128)(2,1)S(1)}, bf16[512,640]{1,0:T(8,128)(2,1)S(1)}, u32[]{:S(2)}, u32[]{:S(2)}) collective-permute-start(bf16[512,640]{1,0:T(8,128)(2,1)S(1)} %get-tuple-element.52), channel_id=1, source_target_pairs={{0,8},{4,12},{8,16},{12,20},{16,24},{20,28},{1,9},{5,13},{9,17},{1... | collective-permute-start | bytes 1966088 | tf_op jit(solution)/shard_map/ppermute | solution.py:306
  26.4 7.7 %collective-permute-done = bf16[512,640]{1,0:T(8,128)(2,1)S(1)} collective-permute-done((bf16[512,640]{1,0:T(8,128)(2,1)}, bf16[512,640]{1,0:T(8,128)(2,1)S(1)}, u32[]{:S(2)}, u32[]{:S(2)}) %collective-permute-start) | collective-permute-done | bytes 655392 | tf_op jit(solution)/shard_map/ppermute | solution.py:303
  44.5 3.5 %collective-permute-start.10 = (bf16[320,640]{1,0:T(8,128)(2,1)S(1)}, bf16[320,640]{1,0:T(8,128)(2,1)S(1)}, u32[]{:S(2)}, u32[]{:S(2)}) collective-permute-start(bf16[320,640]{1,0:T(8,128)(2,1)S(1)} %get-tuple-element.58), channel_id=1, source_target_pairs={{0,8},{4,12},{24,16},{28,20},{1,9},{5,13},{25,17},{29,21},{2,10},{... | collective-permute-start | bytes 1228808 | tf_op jit(solution)/shard_map/ppermute | solution.py:306
  57.9 6.4 %collective-permute-done.5 = bf16[320,640]{1,0:T(8,128)(2,1)S(1)} collective-permute-done((bf16[320,640]{1,0:T(8,128)(2,1)S(1)}, bf16[320,640]{1,0:T(8,128)(2,1)S(1)}, u32[]{:S(2)}, u32[]{:S(2)}) %collective-permute-start.5) | collective-permute-done | bytes 409632 | tf_op jit(solution)/shard_map/ppermute | solution.py:306
  67.6 7.9 %collective-permute-start.8 = (bf16[320,640]{1,0:T(8,128)(2,1)S(1)}, bf16[320,640]{1,0:T(8,128)(2,1)S(1)}, u32[]{:S(2)}, u32[]{:S(2)}) collective-permute-start(bf16[320,640]{1,0:T(8,128)(2,1)S(1)} %convert_element_type.130), channel_id=1, source_target_pairs={{16,24},{20,28},{0,8},{4,12},{17,25},{21,29},{1,9},{5,13},{18,26},... | collective-permute-start | bytes 1228808 | tf_op jit(solution)/shard_map/ppermute | solution.py:306
  77.1 5.3 %collective-permute-start.13 = (bf16[320,640]{1,0:T(8,128)(2,1)S(1)}, bf16[320,640]{1,0:T(8,128)(2,1)S(1)}, u32[]{:S(2)}, u32[]{:S(2)}) collective-permute-start(bf16[320,640]{1,0:T(8,128)(2,1)S(1)} %convert_element_type.140), channel_id=1, source_target_pairs={{16,24},{20,28},{0,8},{4,12},{17,25},{21,29},{1,9},{5,13},{18,26},... | collective-permute-start | bytes 1228808 | tf_op jit(solution)/shard_map/ppermute | solution.py:306
  82.7 17.5 %collective-permute-done.6 = bf16[320,640]{1,0:T(8,128)(2,1)S(1)} collective-permute-done((bf16[320,640]{1,0:T(8,128)(2,1)S(1)}, bf16[320,640]{1,0:T(8,128)(2,1)S(1)}, u32[]{:S(2)}, u32[]{:S(2)}) %collective-permute-start.6) | collective-permute-done | bytes 409632 | tf_op jit(solution)/shard_map/ppermute | solution.py:306
  101.4 6.0 %collective-permute-done.11 = bf16[320,640]{1,0:T(8,128)(2,1)S(1)} collective-permute-done((bf16[320,640]{1,0:T(8,128)(2,1)S(1)}, bf16[320,640]{1,0:T(8,128)(2,1)S(1)}, u32[]{:S(2)}, u32[]{:S(2)}) %collective-permute-start.11) | collective-permute-done | bytes 409632 | tf_op jit(solution)/shard_map/ppermute | solution.py:306
  112.7 8.1 %collective-permute-done.12 = bf16[320,640]{1,0:T(8,128)(2,1)S(1)} collective-permute-done((bf16[320,640]{1,0:T(8,128)(2,1)S(1)}, bf16[320,640]{1,0:T(8,128)(2,1)S(1)}, u32[]{:S(2)}, u32[]{:S(2)}) %collective-permute-start.12) | collective-permute-done | bytes 409632 | tf_op jit(solution)/shard_map/ppermute | solution.py:306
  121.1 4.1 %collective-permute-done.7 = bf16[320,640]{1,0:T(8,128)(2,1)S(1)} collective-permute-done((bf16[320,640]{1,0:T(8,128)(2,1)S(1)}, bf16[320,640]{1,0:T(8,128)(2,1)S(1)}, u32[]{:S(2)}, u32[]{:S(2)}) %collective-permute-start.7) | collective-permute-done | bytes 409632 | tf_op jit(solution)/shard_map/ppermute | solution.py:306
  125.5 5.5 %collective-permute-start.21 = (bf16[512,640]{1,0:T(8,128)(2,1)S(1)}, bf16[512,640]{1,0:T(8,128)(2,1)S(1)}, u32[]{:S(2)}, u32[]{:S(2)}) collective-permute-start(bf16[512,640]{1,0:T(8,128)(2,1)S(1)} %broadcast_select_fusion.4), channel_id=1, source_target_pairs={{0,8},{4,12},{8,16},{12,20},{16,24},{20,28},{1,9},{5,13},{9,17},{1... | collective-permute-start | bytes 1966088 | tf_op jit(solution)/shard_map/ppermute | solution.py:306
  131.1 8.1 %shard_map.92 = bf16[640,640]{1,0:T(8,128)(2,1)S(1)} custom-call(s32[1]{0:T(128)} %bitcast.5.active_ref, f32[640,640]{1,0:T(8,128)S(1)} %pad_maximum_fusion.grad_ref, bf16[640,640]{1,0:T(8,128)(2,1)S(1)} %bitcast_select_fusion.init_ref), custom_call_target="tpu_custom_call" | custom-call | flops 4718592000 | bytes 3276800 | tf_op jit(solution)/shard_map/pallas_call | solution.py:163
  143.3 5.3 %collective-permute-start.19 = (bf16[320,640]{1,0:T(8,128)(2,1)S(1)}, bf16[320,640]{1,0:T(8,128)(2,1)S(1)}, u32[]{:S(2)}, u32[]{:S(2)}) collective-permute-start(bf16[320,640]{1,0:T(8,128)(2,1)S(1)} %slice.47), channel_id=1, source_target_pairs={{0,16},{4,20},{24,8},{28,12},{1,17},{5,21},{25,9},{29,13},{2,18},{... | collective-permute-start | bytes 1228808 | tf_op jit(solution)/shard_map/ppermute | solution.py:306
  148.6 5.6 %collective-permute-done.18 = bf16[320,640]{1,0:T(8,128)(2,1)S(1)} collective-permute-done((bf16[320,640]{1,0:T(8,128)(2,1)S(1)}, bf16[320,640]{1,0:T(8,128)(2,1)S(1)}, u32[]{:S(2)}, u32[]{:S(2)}) %collective-permute-start.18) | collective-permute-done | bytes 409632 | tf_op jit(solution)/shard_map/ppermute | solution.py:306
  154.4 4.4 %collective-permute-start.22 = (bf16[320,640]{1,0:T(8,128)(2,1)S(1)}, bf16[320,640]{1,0:T(8,128)(2,1)S(1)}, u32[]{:S(2)}, u32[]{:S(2)}) collective-permute-start(bf16[320,640]{1,0:T(8,128)(2,1)S(1)} %get-tuple-element.33), channel_id=1, source_target_pairs={{0,8},{4,12},{24,16},{28,20},{1,9},{5,13},{25,17},{29,21},{2,10},{... | collective-permute-start | bytes 1228808 | tf_op jit(solution)/shard_map/ppermute | solution.py:306
  163.4 6.3 %collective-permute-done.22 = bf16[320,640]{1,0:T(8,128)(2,1)S(1)} collective-permute-done((bf16[320,640]{1,0:T(8,128)(2,1)S(1)}, bf16[320,640]{1,0:T(8,128)(2,1)S(1)}, u32[]{:S(2)}, u32[]{:S(2)}) %collective-permute-start.22) | collective-permute-done | bytes 409632 | tf_op jit(solution)/shard_map/ppermute | solution.py:306
  171.3 14.2 %shard_map.93.att_ref = f32[1024,640]{1,0:T(8,128)S(1)} custom-call(s32[1]{0:T(128)} %bitcast.12.first_ref, bf16[1024,640]{1,0:T(8,128)(2,1)S(1)} %pad_maximum_fusion.2.q_ref, bf16[512,640]{1,0:T(8,128)(2,1)S(1)} %collective-permute-done.3.kp_ref, bf16[1024,640]{1,0:T(8,128)(2,1)S(1)} %pad_maximum_fusion.3.k_ref, ...), custom_call_target="tpu_custom_call" | custom-call | flops 1677721600 | bytes 7864320 | tf_op jit(solution)/shard_map/pallas_call | solution.py:111
  193.2 8.6 %collective-permute-done.30.refs_2_ = bf16[512,640]{1,0:T(8,128)(2,1)} collective-permute-done((bf16[512,640]{1,0:T(8,128)(2,1)S(1)}, bf16[512,640]{1,0:T(8,128)(2,1)}, u32[]{:S(2)}, u32[]{:S(2)}) %collective-permute-start.30) | collective-permute-done | bytes 655392 | tf_op jit(solution)/shard_map/ppermute | solution.py:448
  204.3 4.7 %copy-done.2 = bf16[5120,1280]{1,0:T(8,128)(2,1)S(1)} copy-done((bf16[5120,1280]{1,0:T(8,128)(2,1)S(1)}, bf16[5120,1280]{1,0:T(8,128)(2,1)}, u32[]{:S(2)}) %copy-start.2) | copy-done | bytes 13107224
  209.0 6.9 %shard_map.96.refs_6_ = f32[512,1280]{1,0:T(8,128)S(1)} custom-call(s32[4]{0:T(128)S(1)} %pad_add_fusion.1.refs_0_, bf16[512,640]{1,0:T(8,128)(2,1)S(1)} %shard_map.95.refs_1_, bf16[512,640]{1,0:T(8,128)(2,1)} %collective-permute-done.30.refs_2_, bf16[512,640]{1,0:T(8,128)(2,1)} %collective-permute-done.31.refs_3_, ...), custom_call_target="tpu_custom_call" | custom-call | flops 3355443200 | bytes 14417920 | tf_op jit(solution)/shard_map/pallas_call | solution.py:250
  221.9 4.7 %copy-done.3 = bf16[5120,1280]{1,0:T(8,128)(2,1)S(1)} copy-done((bf16[5120,1280]{1,0:T(8,128)(2,1)S(1)}, bf16[5120,1280]{1,0:T(8,128)(2,1)}, u32[]{:S(2)}) %copy-start.3) | copy-done | bytes 13107224
  230.6 6.6 %shard_map.97 = bf16[512,1280]{1,0:T(8,128)(2,1)} custom-call(s32[4]{0:T(128)S(1)} %pad_add_fusion.refs_0_, bf16[512,640]{1,0:T(8,128)(2,1)S(1)} %collective-permute-done.28.refs_1_, bf16[512,640]{1,0:T(8,128)(2,1)S(1)} %collective-permute-done.29.refs_2_, bf16[512,640]{1,0:T(8,128)(2,1)S(1)} %copy-done.7, bf16[512,640]{1,0:T(8,128)(2,1)S(1)} %copy-done.9, ...), custom_call_target="tpu_custom_call" | custom-call | flops 3355443200 | bytes 14417920 | tf_op jit(solution)/shard_map/pallas_call | solution.py:250
  (158 shorter events, 78.1 us)
Async XLA Ops:
  2.1 18.8 %collective-permute-start.2 = (bf16[512,640]{1,0:T(8,128)(2,1)}, bf16[512,640]{1,0:T(8,128)(2,1)}, u32[]{:S(2)}, u32[]{:S(2)}) collective-permute-start(bf16[512,640]{1,0:T(8,128)(2,1)} %constant_dynamic-slice_fusion.2), channel_id=1, source_target_pairs={{0,4},{4,0},{8,12},{12,8},{16,20},{20,16},{24,28},{28,24},{1,5},{5... | collective-permute-start | bytes 1966088 | tf_op jit(solution)/shard_map/ppermute | solution.py:303
  6.0 28.1 %collective-permute-start = (bf16[512,640]{1,0:T(8,128)(2,1)}, bf16[512,640]{1,0:T(8,128)(2,1)S(1)}, u32[]{:S(2)}, u32[]{:S(2)}) collective-permute-start(bf16[512,640]{1,0:T(8,128)(2,1)} %constant_dynamic-slice_fusion.5), channel_id=1, source_target_pairs={{0,4},{4,0},{8,12},{12,8},{16,20},{20,16},{24,28},{28,24},{1,5},{5... | collective-permute-start | bytes 1966088 | tf_op jit(solution)/shard_map/ppermute | solution.py:303
  6.0 37.5 %collective-permute-start.4 = (f32[512]{0:T(512)S(1)}, f32[512]{0:T(512)S(1)}, u32[]{:S(2)}, u32[]{:S(2)}) collective-permute-start(f32[512]{0:T(512)S(1)} %bitcast.45), channel_id=1, source_target_pairs={{0,4},{4,0},{8,12},{12,8},{16,20},{20,16},{24,28},{28,24},{1,5},{5... | collective-permute-start | bytes 6152 | tf_op jit(solution)/shard_map/ppermute | solution.py:303
  22.3 20.4 %collective-permute-start.3 = (bf16[512,640]{1,0:T(8,128)(2,1)S(1)}, bf16[512,640]{1,0:T(8,128)(2,1)S(1)}, u32[]{:S(2)}, u32[]{:S(2)}) collective-permute-start(bf16[512,640]{1,0:T(8,128)(2,1)S(1)} %get-tuple-element.52), channel_id=1, source_target_pairs={{0,8},{4,12},{8,16},{12,20},{16,24},{20,28},{1,9},{5,13},{9,17},{1... | collective-permute-start | bytes 1966088 | tf_op jit(solution)/shard_map/ppermute | solution.py:306
  34.1 41.4 %collective-permute-start.1 = (bf16[512,640]{1,0:T(8,128)(2,1)S(1)}, bf16[512,640]{1,0:T(8,128)(2,1)S(1)}, u32[]{:S(2)}, u32[]{:S(2)}) collective-permute-start(bf16[512,640]{1,0:T(8,128)(2,1)S(1)} %copy-done.18), channel_id=1, source_target_pairs={{0,4},{4,0},{8,12},{12,8},{16,20},{20,16},{24,28},{28,24},{1,5},{5... | collective-permute-start | bytes 1966088 | tf_op jit(solution)/shard_map/ppermute | solution.py:303
  48.1 16.3 %collective-permute-start.5 = (bf16[320,640]{1,0:T(8,128)(2,1)S(1)}, bf16[320,640]{1,0:T(8,128)(2,1)S(1)}, u32[]{:S(2)}, u32[]{:S(2)}) collective-permute-start(bf16[320,640]{1,0:T(8,128)(2,1)S(1)} %get-tuple-element.57), channel_id=1, source_target_pairs={{0,8},{4,12},{24,16},{28,20},{1,9},{5,13},{25,17},{29,21},{2,10},{... | collective-permute-start | bytes 1228808 | tf_op jit(solution)/shard_map/ppermute | solution.py:306
  65.4 17.1 %collective-permute-start.16 = (bf16[320,640]{1,0:T(8,128)(2,1)S(1)}, bf16[320,640]{1,0:T(8,128)(2,1)S(1)}, u32[]{:S(2)}, u32[]{:S(2)}) collective-permute-start(bf16[320,640]{1,0:T(8,128)(2,1)S(1)} %get-tuple-element.55), channel_id=1, source_target_pairs={{8,16},{12,20},{9,17},{13,21},{10,18},{14,22},{11,19},{15,23}} | collective-permute-start | bytes 1228808 | tf_op jit(solution)/shard_map/ppermute | solution.py:306
  66.3 33.9 %collective-permute-start.6 = (bf16[320,640]{1,0:T(8,128)(2,1)S(1)}, bf16[320,640]{1,0:T(8,128)(2,1)S(1)}, u32[]{:S(2)}, u32[]{:S(2)}) collective-permute-start(bf16[320,640]{1,0:T(8,128)(2,1)S(1)} %convert_element_type.124), channel_id=1, source_target_pairs={{16,0},{20,4},{24,8},{28,12},{17,1},{21,5},{25,9},{29,13},{18,2},{... | collective-permute-start | bytes 1228808 | tf_op jit(solution)/shard_map/ppermute | solution.py:306
  67.6 32.7 %collective-permute-start.8 = (bf16[320,640]{1,0:T(8,128)(2,1)S(1)}, bf16[320,640]{1,0:T(8,128)(2,1)S(1)}, u32[]{:S(2)}, u32[]{:S(2)}) collective-permute-start(bf16[320,640]{1,0:T(8,128)(2,1)S(1)} %convert_element_type.130), channel_id=1, source_target_pairs={{16,24},{20,28},{0,8},{4,12},{17,25},{21,29},{1,9},{5,13},{18,26},... | collective-permute-start | bytes 1228808 | tf_op jit(solution)/shard_map/ppermute | solution.py:306
  75.5 31.9 %collective-permute-start.11 = (bf16[320,640]{1,0:T(8,128)(2,1)S(1)}, bf16[320,640]{1,0:T(8,128)(2,1)S(1)}, u32[]{:S(2)}, u32[]{:S(2)}) collective-permute-start(bf16[320,640]{1,0:T(8,128)(2,1)S(1)} %convert_element_type.136), channel_id=1, source_target_pairs={{16,0},{20,4},{24,8},{28,12},{17,1},{21,5},{25,9},{29,13},{18,2},{... | collective-permute-start | bytes 1228808 | tf_op jit(solution)/shard_map/ppermute | solution.py:306
  77.1 31.7 %collective-permute-start.13 = (bf16[320,640]{1,0:T(8,128)(2,1)S(1)}, bf16[320,640]{1,0:T(8,128)(2,1)S(1)}, u32[]{:S(2)}, u32[]{:S(2)}) collective-permute-start(bf16[320,640]{1,0:T(8,128)(2,1)S(1)} %convert_element_type.140), channel_id=1, source_target_pairs={{16,24},{20,28},{0,8},{4,12},{17,25},{21,29},{1,9},{5,13},{18,26},... | collective-permute-start | bytes 1228808 | tf_op jit(solution)/shard_map/ppermute | solution.py:306
  109.8 15.3 %collective-permute-start.7 = (bf16[320,640]{1,0:T(8,128)(2,1)S(1)}, bf16[320,640]{1,0:T(8,128)(2,1)S(1)}, u32[]{:S(2)}, u32[]{:S(2)}) collective-permute-start(bf16[320,640]{1,0:T(8,128)(2,1)S(1)} %get-tuple-element.47), channel_id=1, source_target_pairs={{8,0},{12,4},{9,1},{13,5},{10,2},{14,6},{11,3},{15,7}} | collective-permute-start | bytes 1228808 | tf_op jit(solution)/shard_map/ppermute | solution.py:306
  112.0 19.0 %collective-permute-start.17 = (bf16[320,640]{1,0:T(8,128)(2,1)S(1)}, bf16[320,640]{1,0:T(8,128)(2,1)S(1)}, u32[]{:S(2)}, u32[]{:S(2)}) collective-permute-start(bf16[320,640]{1,0:T(8,128)(2,1)S(1)} %get-tuple-element.66), channel_id=1, source_target_pairs={{16,8},{20,12},{17,9},{21,13},{18,10},{22,14},{19,11},{23,15}} | collective-permute-start | bytes 1228808 | tf_op jit(solution)/shard_map/ppermute | solution.py:306
  125.5 28.9 %collective-permute-start.21 = (bf16[512,640]{1,0:T(8,128)(2,1)S(1)}, bf16[512,640]{1,0:T(8,128)(2,1)S(1)}, u32[]{:S(2)}, u32[]{:S(2)}) collective-permute-start(bf16[512,640]{1,0:T(8,128)(2,1)S(1)} %broadcast_select_fusion.4), channel_id=1, source_target_pairs={{0,8},{4,12},{8,16},{12,20},{16,24},{20,28},{1,9},{5,13},{9,17},{1... | collective-permute-start | bytes 1966088 | tf_op jit(solution)/shard_map/ppermute | solution.py:306
  139.2 15.1 %collective-permute-start.18 = (bf16[320,640]{1,0:T(8,128)(2,1)S(1)}, bf16[320,640]{1,0:T(8,128)(2,1)S(1)}, u32[]{:S(2)}, u32[]{:S(2)}) collective-permute-start(bf16[320,640]{1,0:T(8,128)(2,1)S(1)} %slice.47), channel_id=1, source_target_pairs={{0,8},{4,12},{24,16},{28,20},{1,9},{5,13},{25,17},{29,21},{2,10},{... | collective-permute-start | bytes 1228808 | tf_op jit(solution)/shard_map/ppermute | solution.py:306
  140.6 18.2 %collective-permute-start.27 = (bf16[320,640]{1,0:T(8,128)(2,1)S(1)}, bf16[320,640]{1,0:T(8,128)(2,1)S(1)}, u32[]{:S(2)}, u32[]{:S(2)}) collective-permute-start(bf16[320,640]{1,0:T(8,128)(2,1)S(1)} %get-tuple-element.65), channel_id=1, source_target_pairs={{8,0},{12,4},{16,24},{20,28},{9,1},{13,5},{17,25},{21,29},{10,2},{... | collective-permute-start | bytes 1228808 | tf_op jit(solution)/shard_map/ppermute | solution.py:306
  142.0 21.3 %collective-permute-start.25 = (bf16[320,640]{1,0:T(8,128)(2,1)S(1)}, bf16[320,640]{1,0:T(8,128)(2,1)S(1)}, u32[]{:S(2)}, u32[]{:S(2)}) collective-permute-start(bf16[320,640]{1,0:T(8,128)(2,1)S(1)} %broadcast_select_fusion.9), channel_id=1, source_target_pairs={{8,0},{12,4},{16,24},{20,28},{9,1},{13,5},{17,25},{21,29},{10,2},{... | collective-permute-start | bytes 1228808 | tf_op jit(solution)/shard_map/ppermute | solution.py:306
  143.3 42.3 %collective-permute-start.19 = (bf16[320,640]{1,0:T(8,128)(2,1)S(1)}, bf16[320,640]{1,0:T(8,128)(2,1)S(1)}, u32[]{:S(2)}, u32[]{:S(2)}) collective-permute-start(bf16[320,640]{1,0:T(8,128)(2,1)S(1)} %slice.47), channel_id=1, source_target_pairs={{0,16},{4,20},{24,8},{28,12},{1,17},{5,21},{25,9},{29,13},{2,18},{... | collective-permute-start | bytes 1228808 | tf_op jit(solution)/shard_map/ppermute | solution.py:306
  154.4 15.4 %collective-permute-start.22 = (bf16[320,640]{1,0:T(8,128)(2,1)S(1)}, bf16[320,640]{1,0:T(8,128)(2,1)S(1)}, u32[]{:S(2)}, u32[]{:S(2)}) collective-permute-start(bf16[320,640]{1,0:T(8,128)(2,1)S(1)} %get-tuple-element.33), channel_id=1, source_target_pairs={{0,8},{4,12},{24,16},{28,20},{1,9},{5,13},{25,17},{29,21},{2,10},{... | collective-permute-start | bytes 1228808 | tf_op jit(solution)/shard_map/ppermute | solution.py:306
  158.8 26.9 %collective-permute-start.23 = (bf16[320,640]{1,0:T(8,128)(2,1)S(1)}, bf16[320,640]{1,0:T(8,128)(2,1)S(1)}, u32[]{:S(2)}, u32[]{:S(2)}) collective-permute-start(bf16[320,640]{1,0:T(8,128)(2,1)S(1)} %get-tuple-element.33), channel_id=1, source_target_pairs={{0,16},{4,20},{24,8},{28,12},{1,17},{5,21},{25,9},{29,13},{2,18},{... | collective-permute-start | bytes 1228808 | tf_op jit(solution)/shard_map/ppermute | solution.py:306
  162.0 23.6 %collective-permute-start.20 = (bf16[320,640]{1,0:T(8,128)(2,1)S(1)}, bf16[320,640]{1,0:T(8,128)(2,1)S(1)}, u32[]{:S(2)}, u32[]{:S(2)}) collective-permute-start(bf16[320,640]{1,0:T(8,128)(2,1)S(1)} %get-tuple-element.67), channel_id=1, source_target_pairs={{8,24},{12,28},{16,0},{20,4},{9,25},{13,29},{17,1},{21,5},{10,26},... | collective-permute-start | bytes 1228808 | tf_op jit(solution)/shard_map/ppermute | solution.py:306
  169.8 15.9 %collective-permute-start.24 = (bf16[320,640]{1,0:T(8,128)(2,1)S(1)}, bf16[320,640]{1,0:T(8,128)(2,1)S(1)}, u32[]{:S(2)}, u32[]{:S(2)}) collective-permute-start(bf16[320,640]{1,0:T(8,128)(2,1)S(1)} %broadcast_select_fusion.11), channel_id=1, source_target_pairs={{8,24},{12,28},{16,0},{20,4},{9,25},{13,29},{17,1},{21,5},{10,26},... | collective-permute-start | bytes 1228808 | tf_op jit(solution)/shard_map/ppermute | solution.py:306
  203.2 15.8 %collective-permute-start.29 = (bf16[512,640]{1,0:T(8,128)(2,1)S(1)}, bf16[512,640]{1,0:T(8,128)(2,1)S(1)}, u32[]{:S(2)}, u32[]{:S(2)}) collective-permute-start(bf16[512,640]{1,0:T(8,128)(2,1)S(1)} %collective-permute-done.28.refs_1_), channel_id=1, source_target_pairs={{0,2},{1,3},{2,0},{3,1},{4,6},{5,7},{6,4},{7,5},{8,10},{9,11},{10,... | collective-permute-start | bytes 1966088 | tf_op jit(solution)/shard_map/ppermute | solution.py:448
  203.8 15.2 %collective-permute-start.33 = (bf16[512,640]{1,0:T(8,128)(2,1)S(1)}, bf16[512,640]{1,0:T(8,128)(2,1)S(1)}, u32[]{:S(2)}, u32[]{:S(2)}) collective-permute-start(bf16[512,640]{1,0:T(8,128)(2,1)S(1)} %collective-permute-done.28.refs_1_), channel_id=1, source_target_pairs={{0,1},{1,0},{2,3},{3,2},{4,5},{5,4},{6,7},{7,6},{8,9},{9,8},{10,11... | collective-permute-start | bytes 1966088 | tf_op jit(solution)/shard_map/ppermute | solution.py:448
  (33 other events, 198.3 us)
